TPU v7x, 256 devices: a whole 4x4x8 slice. The times are simulated.
256 devices in a mesh: dp: 8 (over x, core), cluster: 32 (over z, y).
Axes of the slice: x: 4, y: 4, z: 8, core: 2. Of those that a mesh axis runs over, the one named last changes fastest.
Arguments:
- points: bfloat16 [2, 65536, 1024], P(None, ('dp', 'cluster')), may hold values from -400 to 400
- candidates: int32 [2, 2048, 4], P(None, ('dp', 'cluster')), may hold values from 0 to 31, all different within a row; in each aligned block of 8 rows (0 to 7, 8 to 15, ..., all dimensions but the last counted through in order) at most 2 rows name the same one
- centroids: bfloat16 [16384, 1024], P('cluster'), may hold values from -0.1875 to 0.1875
Outputs:
- final_sums: float32 [16384, 1024], P('cluster', 'dp')
- final_counts: float32 [16384], P('cluster')
Inputs may be any that keep to these rules, and one draw needn't show every extreme that they name: `candidates`: each row names 4 different centroid blocks. In the 8 aligned rows of one step that belong to one device, no block is named more than 2 times, and in some such blocks of rows one block is named exactly 2 times.
All inputs are finite; a program needn't handle non-finite values.
Results may differ from a plain program's by a relative error of at most 0.015.
The roundings to bfloat16 on the way count: a program that leaves them out, or rounds other values in their place, can miss the bound.
Values may be sent and summed in bfloat16 or wider, within the bound.
A program may use at most 64 MiB of HBM per device.

v0:
```python
import jax
import jax.numpy as jnp
from jax import lax
from jax.sharding import PartitionSpec as P


def normalize_rows(vectors):
    return vectors / jnp.sqrt(jnp.sum(vectors * vectors, axis=1, keepdims=True) + 1e-06)


def routing(step_cands, n_owner, slot_cap):
    blocks_here, cand_count = step_cands.shape
    owner_ids = step_cands.reshape(-1)
    owner_hits = (owner_ids[:, None] == jnp.arange(n_owner, dtype=jnp.int32)[None, :]).astype(
        jnp.int32
    )
    earlier = jnp.cumsum(owner_hits, axis=0) - owner_hits
    position = jnp.sum(earlier * owner_hits, axis=1)
    slot_index = owner_ids * slot_cap + position
    to_slot = (
        slot_index[:, None] == jnp.arange(n_owner * slot_cap, dtype=jnp.int32)[None, :]
    ).astype(jnp.float32)
    pair_block = jnp.arange(blocks_here * cand_count, dtype=jnp.int32) // cand_count
    block_of = (pair_block[:, None] == jnp.arange(blocks_here, dtype=jnp.int32)[None, :]).astype(
        jnp.float32
    )
    dispatch = jnp.dot(to_slot.T, block_of, precision=lax.Precision.HIGHEST).astype(jnp.bfloat16)
    return (to_slot, dispatch)


def score_rows(arrived_rows, centroid_rows):
    return jnp.einsum("rd,cd->rc", arrived_rows, centroid_rows, preferred_element_type=jnp.float32)


def owner_sums(arrived, centroid_rows, to_slot, cand_count):
    n_owner, slot_cap, rows_block, feature_width = arrived.shape
    highest = lax.Precision.HIGHEST
    arrived_rows = arrived.reshape(-1, feature_width)
    scores = score_rows(arrived_rows, centroid_rows)
    row_max = jnp.max(scores, axis=1)
    row_total = jnp.sum(jnp.exp(scores - row_max[:, None]), axis=1)
    back_max, back_total = (
        lax.all_to_all(
            row_max.reshape(n_owner, slot_cap, rows_block),
            "cluster",
            split_axis=0,
            concat_axis=0,
            tiled=True,
        ),
        lax.all_to_all(
            row_total.reshape(n_owner, slot_cap, rows_block),
            "cluster",
            split_axis=0,
            concat_axis=0,
            tiled=True,
        ),
    )
    blocks_here = to_slot.shape[0] // cand_count
    pair_max = jnp.dot(to_slot, back_max.reshape(-1, rows_block), precision=highest).reshape(
        blocks_here, cand_count, rows_block
    )
    pair_total = jnp.dot(to_slot, back_total.reshape(-1, rows_block), precision=highest).reshape(
        blocks_here, cand_count, rows_block
    )
    point_max = jnp.max(pair_max, axis=1, keepdims=True)
    point_total = jnp.sum(pair_total * jnp.exp(pair_max - point_max), axis=1, keepdims=True)
    pair_shift = jnp.broadcast_to(point_max, pair_max.shape).reshape(-1, rows_block)
    pair_scale = jnp.broadcast_to(1.0 / point_total, pair_max.shape).reshape(-1, rows_block)
    slot_shift = jnp.dot(to_slot.T, pair_shift, precision=highest)
    slot_scale = jnp.dot(to_slot.T, pair_scale, precision=highest)
    got_shift, got_scale = (
        lax.all_to_all(
            slot_shift.reshape(n_owner, slot_cap, rows_block),
            "cluster",
            split_axis=0,
            concat_axis=0,
            tiled=True,
        ),
        lax.all_to_all(
            slot_scale.reshape(n_owner, slot_cap, rows_block),
            "cluster",
            split_axis=0,
            concat_axis=0,
            tiled=True,
        ),
    )
    weights = (
        jnp.exp(scores - got_shift.reshape(-1)[:, None]) * got_scale.reshape(-1)[:, None]
    ).astype(jnp.bfloat16)
    block_sums = jnp.einsum("rc,rd->cd", weights, arrived_rows, preferred_element_type=jnp.float32)
    block_counts = jnp.sum(weights, axis=0, dtype=jnp.float32)
    return (block_sums, block_counts)


def on_device(points, candidates, centroids):
    n_owner = lax.axis_size("cluster")
    steps_total, blocks_here, cand_count = candidates.shape
    rows_block = points.shape[1] // blocks_here
    feature_width = points.shape[2]
    slot_cap = max(2, 2 * blocks_here * cand_count // n_owner)
    routed = [
        routing(candidates[step_index], n_owner, slot_cap) for step_index in range(steps_total)
    ]
    outgoing = [
        jnp.dot(
            routed[step_index][1],
            points[step_index].reshape(blocks_here, rows_block * feature_width),
            preferred_element_type=jnp.float32,
        )
        .astype(jnp.bfloat16)
        .reshape(n_owner, slot_cap, rows_block, feature_width)
        for step_index in range(steps_total)
    ]
    arrivals = [
        lax.all_to_all(message, "cluster", split_axis=0, concat_axis=0, tiled=True)
        for message in outgoing
    ]
    current = centroids
    for step_index in range(steps_total):
        block_sums, block_counts = owner_sums(
            arrivals[step_index], current, routed[step_index][0], cand_count
        )
        if step_index + 1 < steps_total:
            summed = lax.psum(block_sums, "dp")
            current = normalize_rows(current.astype(jnp.float32) + summed).astype(jnp.bfloat16)
    final_sums = lax.psum_scatter(
        block_sums.astype(jnp.bfloat16), "dp", scatter_dimension=1, tiled=True
    ).astype(jnp.float32)
    final_counts = lax.psum(block_counts, "dp")
    return (final_sums, final_counts)


def solution(mesh):
    placed = (
        P(None, ("dp", "cluster"), None),
        P(None, ("dp", "cluster"), None),
        P("cluster", None),
    )
    return jax.shard_map(
        on_device,
        mesh=mesh,
        in_specs=placed,
        out_specs=(P("cluster", "dp"), P("cluster")),
        check_vma=False,
    )
```

profile of v0, /device:TPU:2, one launch (start us, length us, event | category | flops | bytes accessed | tf_op | source)
XLA Modules:
  0.0 392.0 jit_solution(15684706378504997939)
XLA Ops:
  11.9 4.4 %copy.50 = bf16[8,8,32,1024]{3,2,1,0:T(8,128)(2,1)} copy(bf16[8,8,32,1024]{3,1,2,0:T(8,128)(2,1)S(1)} %bitcast.69) | data formatting | bytes 8388608
  16.3 11.7 %all-to-all-start.1 = ((bf16[32,2,32,1024]{3,2,1,0:T(8,128)(2,1)}), bf16[32,2,32,1024]{3,2,1,0:T(8,128)(2,1)}, u32[]{:S(2)}, u32[]{:S(2)}) async-start(bf16[32,2,32,1024]{3,2,1,0:T(8,128)(2,1)} %bitcast.68), calls=%async_computation.1 | async-start | bytes 8388608 | tf_op jit(solution)/shard_map/all_to_all | solution.py:115
  28.9 93.5 %all-to-all-done.1 = bf16[32,2,32,1024]{3,2,1,0:T(8,128)(2,1)} async-done(((bf16[32,2,32,1024]{3,2,1,0:T(8,128)(2,1)}), bf16[32,2,32,1024]{3,2,1,0:T(8,128)(2,1)}, u32[]{:S(2)}, u32[]{:S(2)}) %all-to-all-start.1) | async-done | bytes 4194336 | tf_op jit(solution)/shard_map/all_to_all | solution.py:115
  122.4 6.5 %fusion.43 = (f32[2048]{0:T(1024)S(1)}, f32[2048,512]{0,1:T(8,128)}) fusion(bf16[2048,1024]{1,0:T(8,128)(2,1)} %bitcast.1, bf16[512,1024]{1,0:T(8,128)(2,1)S(1)} %copy-done), kind=kOutput, calls=%fused_computation.75 | convolution fusion | flops 2148530176 | bytes 9445376 | tf_op jit(solution)/shard_map/rd,cd->rc/dot_general | solution.py:32
  129.7 6.8 %all-to-all-start.2 = ((f32[32,2,32]{2,1,0:T(2,128)}), f32[32,2,32]{2,1,0:T(2,128)S(1)}, u32[]{:S(2)}, u32[]{:S(2)}) async-start(f32[32,2,32]{2,1,0:T(2,128)} %reshape.231), calls=%async_computation.2 | async-start | bytes 65536 | tf_op jit(solution)/shard_map/all_to_all | solution.py:43
  139.9 6.3 %all-to-all-done.2 = f32[32,2,32]{2,1,0:T(2,128)S(1)} async-done(((f32[32,2,32]{2,1,0:T(2,128)}), f32[32,2,32]{2,1,0:T(2,128)S(1)}, u32[]{:S(2)}, u32[]{:S(2)}) %all-to-all-start.2) | async-done | bytes 8224 | tf_op jit(solution)/shard_map/all_to_all | solution.py:43
  150.3 9.6 %all-to-all-done.4 = f32[32,2,32]{2,1,0:T(2,128)S(1)} async-done(((f32[32,2,32]{2,1,0:T(2,128)}), f32[32,2,32]{2,1,0:T(2,128)S(1)}, u32[]{:S(2)}, u32[]{:S(2)}) %all-to-all-start.4) | async-done | bytes 8224 | tf_op jit(solution)/shard_map/all_to_all | solution.py:50
  165.7 8.9 %all-to-all-done.5 = f32[32,2,32]{2,1,0:T(2,128)S(1)} async-done(((f32[32,2,32]{2,1,0:T(2,128)}), f32[32,2,32]{2,1,0:T(2,128)S(1)}, u32[]{:S(2)}, u32[]{:S(2)}) %all-to-all-start.5) | async-done | bytes 8224 | tf_op jit(solution)/shard_map/all_to_all | solution.py:79
  174.6 4.0 %all-to-all-start.3 = ((f32[32,2,32]{2,1,0:T(2,128)}), f32[32,2,32]{2,1,0:T(2,128)S(1)}, u32[]{:S(2)}, u32[]{:S(2)}) async-start(f32[32,2,32]{2,1,0:T(2,128)} %copy.28), calls=%async_computation.3 | async-start | bytes 65536 | tf_op jit(solution)/shard_map/all_to_all | solution.py:72
  179.9 4.4 %copy.49 = bf16[8,8,32,1024]{3,2,1,0:T(8,128)(2,1)} copy(bf16[8,8,32,1024]{3,1,2,0:T(8,128)(2,1)S(1)} %bitcast.70) | data formatting | bytes 8388608
  184.4 3.9 all-to-all-done.3
  188.2 5.8 %all-to-all-start = ((bf16[32,2,32,1024]{3,2,1,0:T(8,128)(2,1)}), bf16[32,2,32,1024]{3,2,1,0:T(8,128)(2,1)}, u32[]{:S(2)}, u32[]{:S(2)}) async-start(bf16[32,2,32,1024]{3,2,1,0:T(8,128)(2,1)} %bitcast.67), calls=%async_computation | async-start | bytes 8388608 | tf_op jit(solution)/shard_map/all_to_all | solution.py:115
  194.3 7.2 %fusion = f32[512,1024]{1,0:T(8,128)} fusion(bf16[2048,1024]{1,0:T(8,128)(2,1)} %bitcast.1, f32[2048,512]{0,1:T(8,128)} %get-tuple-element.9, f32[2048]{0:T(1024)S(1)} %mul.68, f32[2048]{0:T(1024)S(1)} %sub.67), kind=kOutput, calls=%fused_computation.7 | convolution fusion | flops 2150629376 | bytes 10502144 | tf_op jit(solution)/shard_map/rc,rd->cd/dot_general | solution.py:90
  201.5 70.9 %all-reduce.2.cloned.1.call-done = f32[512,1024]{1,0:T(8,128)} async-done(((f32[512,1024]{1,0:T(8,128)}), f32[512,1024]{1,0:T(8,128)}) %all-reduce.2.cloned.1.call-update) | async-done | bytes 2097168 | tf_op jit(solution)/shard_map/psum | solution.py:124
  274.3 12.1 %all-to-all-done = bf16[32,2,32,1024]{3,2,1,0:T(8,128)(2,1)} async-done(((bf16[32,2,32,1024]{3,2,1,0:T(8,128)(2,1)}), bf16[32,2,32,1024]{3,2,1,0:T(8,128)(2,1)}, u32[]{:S(2)}, u32[]{:S(2)}) %all-to-all-start) | async-done | bytes 4194336 | tf_op jit(solution)/shard_map/all_to_all | solution.py:115
  286.4 7.2 %fusion.45 = (f32[2048]{0:T(1024)S(1)}, f32[2048,512]{0,1:T(8,128)}) fusion(bf16[2048,1024]{1,0:T(8,128)(2,1)} %bitcast, f32[512,1024]{1,0:T(8,128)} %all-reduce.2.cloned.1.call-done, bf16[512,1024]{1,0:T(8,128)(2,1)S(1)} %copy-done, f32[512]{0:T(512)S(1)} %add_sqrt_fusion), kind=kOutput, calls=%fused_computation.77 | convolution fusion | flops 2150627328 | bytes 11544576 | tf_op jit(solution)/shard_map/rd,cd->rc/dot_general | solution.py:32
  294.3 5.1 %all-to-all-start.6 = ((f32[32,2,32]{2,1,0:T(2,128)}), f32[32,2,32]{2,1,0:T(2,128)S(1)}, u32[]{:S(2)}, u32[]{:S(2)}) async-start(f32[32,2,32]{2,1,0:T(2,128)} %reshape.237), calls=%async_computation.6 | async-start | bytes 65536 | tf_op jit(solution)/shard_map/all_to_all | solution.py:43
  303.0 6.3 %all-to-all-done.6 = f32[32,2,32]{2,1,0:T(2,128)S(1)} async-done(((f32[32,2,32]{2,1,0:T(2,128)}), f32[32,2,32]{2,1,0:T(2,128)S(1)}, u32[]{:S(2)}, u32[]{:S(2)}) %all-to-all-start.6) | async-done | bytes 8224 | tf_op jit(solution)/shard_map/all_to_all | solution.py:43
  314.2 8.7 %all-to-all-done.8 = f32[32,2,32]{2,1,0:T(2,128)S(1)} async-done(((f32[32,2,32]{2,1,0:T(2,128)}), f32[32,2,32]{2,1,0:T(2,128)S(1)}, u32[]{:S(2)}, u32[]{:S(2)}) %all-to-all-start.8) | async-done | bytes 8224 | tf_op jit(solution)/shard_map/all_to_all | solution.py:50
  327.8 8.7 %all-to-all-done.7 = f32[32,2,32]{2,1,0:T(2,128)S(1)} async-done(((f32[32,2,32]{2,1,0:T(2,128)}), f32[32,2,32]{2,1,0:T(2,128)S(1)}, u32[]{:S(2)}, u32[]{:S(2)}) %all-to-all-start.7) | async-done | bytes 8224 | tf_op jit(solution)/shard_map/all_to_all | solution.py:72
  340.7 9.4 %all-to-all-done.9 = f32[32,2,32]{2,1,0:T(2,128)S(1)} async-done(((f32[32,2,32]{2,1,0:T(2,128)}), f32[32,2,32]{2,1,0:T(2,128)S(1)}, u32[]{:S(2)}, u32[]{:S(2)}) %all-to-all-start.9) | async-done | bytes 8224 | tf_op jit(solution)/shard_map/all_to_all | solution.py:79
  350.2 5.8 %convolution_convert_fusion.2 = bf16[512,1024]{1,0:T(8,128)(2,1)S(1)} fusion(bf16[2048,1024]{1,0:T(8,128)(2,1)} %bitcast, f32[2048,512]{0,1:T(8,128)} %get-tuple-element.13, f32[2048]{0:T(1024)S(1)} %mul.75, f32[2048]{0:T(1024)S(1)} %sub.73), kind=kOutput, calls=%fused_computation.13 | convolution fusion | flops 2151153664 | bytes 9453568 | tf_op jit(solution)/shard_map/rc,rd->cd/dot_general | solution.py:90
  360.4 11.0 %psum.15 = f32[512]{0:T(512)} all-reduce(f32[512]{0:T(512)S(1)} %convert_reduce_fusion), channel_id=1, replica_groups=mesh['dp'=8,'cluster'=32] {'dp'}, use_global_device_ids=true, to_apply=%region_16.17 | all-reduce | flops 512 | bytes 4096 | tf_op jit(solution)/shard_map/psum | solution.py:129
  371.4 12.1 %reduce-scatter.4.cloned.1.call-done = bf16[128,512]{1,0:T(8,128)(2,1)} async-done(((bf16[1024,512]{1,0:T(8,128)(2,1)}), bf16[128,512]{1,0:T(8,128)(2,1)}) %reduce-scatter.4.cloned.1.call-update) | async-done | bytes 131088
  (73 shorter events, 47.2 us)
Async XLA Ops:
  16.3 12.6 %copy-start.1 = (s32[2,8,4]{1,2,0:T(4,128)S(1)}, s32[2,8,4]{1,2,0:T(4,128)}, u32[]{:S(2)}) copy-start(s32[2,8,4]{1,2,0:T(4,128)} %param.4) | copy-start | bytes 772
  16.3 106.1 %copy-start = (bf16[512,1024]{1,0:T(8,128)(2,1)S(1)}, bf16[512,1024]{1,0:T(8,128)(2,1)}, u32[]{:S(2)}) copy-start(bf16[512,1024]{1,0:T(8,128)(2,1)} %param.5) | copy-start | bytes 3145732
  16.3 106.1 %all-to-all-start.1 = ((bf16[32,2,32,1024]{3,2,1,0:T(8,128)(2,1)}), bf16[32,2,32,1024]{3,2,1,0:T(8,128)(2,1)}, u32[]{:S(2)}, u32[]{:S(2)}) async-start(bf16[32,2,32,1024]{3,2,1,0:T(8,128)(2,1)} %bitcast.68), calls=%async_computation.1 | async-start | bytes 8388608 | tf_op jit(solution)/shard_map/all_to_all | solution.py:115
  129.7 16.6 %all-to-all-start.2 = ((f32[32,2,32]{2,1,0:T(2,128)}), f32[32,2,32]{2,1,0:T(2,128)S(1)}, u32[]{:S(2)}, u32[]{:S(2)}) async-start(f32[32,2,32]{2,1,0:T(2,128)} %reshape.231), calls=%async_computation.2 | async-start | bytes 65536 | tf_op jit(solution)/shard_map/all_to_all | solution.py:43
  146.2 13.6 %all-to-all-start.4 = ((f32[32,2,32]{2,1,0:T(2,128)}), f32[32,2,32]{2,1,0:T(2,128)S(1)}, u32[]{:S(2)}, u32[]{:S(2)}) async-start(f32[32,2,32]{2,1,0:T(2,128)} %reshape.234), calls=%async_computation.4 | async-start | bytes 65536 | tf_op jit(solution)/shard_map/all_to_all | solution.py:50
  161.0 13.6 %all-to-all-start.5 = ((f32[32,2,32]{2,1,0:T(2,128)}), f32[32,2,32]{2,1,0:T(2,128)S(1)}, u32[]{:S(2)}, u32[]{:S(2)}) async-start(f32[32,2,32]{2,1,0:T(2,128)} %copy.30), calls=%async_computation.5 | async-start | bytes 65536 | tf_op jit(solution)/shard_map/all_to_all | solution.py:79
  174.6 13.6 %all-to-all-start.3 = ((f32[32,2,32]{2,1,0:T(2,128)}), f32[32,2,32]{2,1,0:T(2,128)S(1)}, u32[]{:S(2)}, u32[]{:S(2)}) async-start(f32[32,2,32]{2,1,0:T(2,128)} %copy.28), calls=%async_computation.3 | async-start | bytes 65536 | tf_op jit(solution)/shard_map/all_to_all | solution.py:72
  188.2 98.2 %all-to-all-start = ((bf16[32,2,32,1024]{3,2,1,0:T(8,128)(2,1)}), bf16[32,2,32,1024]{3,2,1,0:T(8,128)(2,1)}, u32[]{:S(2)}, u32[]{:S(2)}) async-start(bf16[32,2,32,1024]{3,2,1,0:T(8,128)(2,1)} %bitcast.67), calls=%async_computation | async-start | bytes 8388608 | tf_op jit(solution)/shard_map/all_to_all | solution.py:115
  194.1 78.3 %all-reduce.2.cloned.1.call-start = ((), (), s32[]{:S(2)}) async-start(), calls=%async_computation.11 | async-start | bytes 4194304 | tf_op jit(solution)/shard_map/psum | solution.py:124
  294.3 15.0 %all-to-all-start.6 = ((f32[32,2,32]{2,1,0:T(2,128)}), f32[32,2,32]{2,1,0:T(2,128)S(1)}, u32[]{:S(2)}, u32[]{:S(2)}) async-start(f32[32,2,32]{2,1,0:T(2,128)} %reshape.237), calls=%async_computation.6 | async-start | bytes 65536 | tf_op jit(solution)/shard_map/all_to_all | solution.py:43
  309.3 13.6 %all-to-all-start.8 = ((f32[32,2,32]{2,1,0:T(2,128)}), f32[32,2,32]{2,1,0:T(2,128)S(1)}, u32[]{:S(2)}, u32[]{:S(2)}) async-start(f32[32,2,32]{2,1,0:T(2,128)} %reshape.240), calls=%async_computation.8 | async-start | bytes 65536 | tf_op jit(solution)/shard_map/all_to_all | solution.py:50
  323.0 13.6 %all-to-all-start.7 = ((f32[32,2,32]{2,1,0:T(2,128)}), f32[32,2,32]{2,1,0:T(2,128)S(1)}, u32[]{:S(2)}, u32[]{:S(2)}) async-start(f32[32,2,32]{2,1,0:T(2,128)} %copy.34), calls=%async_computation.7 | async-start | bytes 65536 | tf_op jit(solution)/shard_map/all_to_all | solution.py:72
  336.5 13.6 %all-to-all-start.9 = ((f32[32,2,32]{2,1,0:T(2,128)}), f32[32,2,32]{2,1,0:T(2,128)S(1)}, u32[]{:S(2)}, u32[]{:S(2)}) async-start(f32[32,2,32]{2,1,0:T(2,128)} %copy.36), calls=%async_computation.9 | async-start | bytes 65536 | tf_op jit(solution)/shard_map/all_to_all | solution.py:79
  340.4 43.0 %reduce-scatter.4.cloned.1.call-start = ((), (), s32[]{:S(2)}) async-start(), calls=%async_computation.12 | async-start | bytes 1179648
Sparse Core Ops, SparseCore 0:
  201.6 70.7 all-reduce.1
  357.5 25.8 reduce-scatter.3
where the time goes:
time: 396 us; the launch traced here: 392 us
  waiting for transfers between devices  250 us (63%)
  starting transfers between devices  53.1 us (13%)
  matrix products  31.4 us (8%)
  local copies, waits for them, and re-layouts  20 us (5%)
  between operations  14.3 us (4%)
  other arithmetic  11.8 us (3%)
  blocking collectives  11 us (3%)
    all_to_all x2, waiting for transfers between devices, on_device(): lax.all_to_all(message, 'cluster', split_axis=0, concat_axis=0, tiled=True)  106 us
    psum x1, waiting for transfers between devices, on_device(): summed = lax.psum(block_sums, 'dp')  70.9 us
    all_to_all x2, waiting for transfers between devices, owner_sums(): lax.all_to_all(slot_scale.reshape(n_owner, slot_cap, rows_block), 'cluste...  18.3 us
    all_to_all x2, waiting for transfers between devices, owner_sums(): lax.all_to_all(row_total.reshape(n_owner, slot_cap, rows_block), 'cluster...  18.3 us
    all_to_all x2, starting transfers between devices, on_device(): lax.all_to_all(message, 'cluster', split_axis=0, concat_axis=0, tiled=True)  17.6 us
    dot_general x2, matrix products, score_rows(): jnp.einsum('rd,cd->rc', arrived_rows, centroid_rows, preferred_element_ty...  13.8 us
    dot_general x2, matrix products, owner_sums(): jnp.einsum('rc,rd->cd', weights, arrived_rows, preferred_element_type=jnp...  13 us
    all_to_all x2, waiting for transfers between devices, owner_sums(): lax.all_to_all(row_max.reshape(n_owner, slot_cap, rows_block), 'cluster',...  12.7 us
  transfers between devices with their start and end apart: 12, of which 12 were waited for; matrix products, arithmetic and copies ran while one was open for 7% of the time, Pallas kernels for 0%

commit v1 on v0

v1 whole, which is shorter than its diff:
```python
import jax
import jax.numpy as jnp
from jax import lax
from jax.experimental import pallas as pl
from jax.experimental.pallas import tpu as pltpu
from jax.sharding import PartitionSpec as P

MESH = pl.DeviceIdType.MESH
F32 = jnp.float32
BF16 = jnp.bfloat16
BIG = 3.0e38
NZ, NY, NX, NC = 8, 4, 4, 2
NB, PB, D, CBS = 8, 32, 1024, 512
PLUS = ((1, 0), (1, 1), (2, 0), (2, 1), (3, 0), (3, 1), (4, 0))
MINUS = ((7, 1), (7, 0), (6, 1), (6, 0), (5, 1), (5, 0), (4, 1))
SCHEDULE = (
    ("zs", 0, 0), ("zs", 0, 1), ("pick", 0, 0), ("relay", 0, 0), ("ze", 0, 0, 0), ("ze", 0, 1, 0), ("score", 0, 0),
    ("ze", 0, 0, 1), ("pick", 0, 1), ("ze", 0, 1, 1), ("pick", 0, 7), ("relay", 0, 1), ("ze", 0, 0, 2),
    ("ze", 0, 1, 2), ("relay", 0, 7), ("ze", 0, 0, 3), ("pick", 0, 2), ("ze", 0, 1, 3), ("pick", 0, 6),
    ("score", 0, 1), ("score", 0, 7), ("relay", 0, 2), ("ze", 0, 0, 4), ("ze", 0, 1, 4), ("relay", 0, 6),
    ("ze", 0, 0, 5), ("pick", 0, 3), ("ze", 0, 1, 5), ("pick", 0, 5), ("score", 0, 2), ("score", 0, 6),
    ("relay", 0, 3), ("ze", 0, 0, 6), ("ze", 0, 1, 6), ("zs", 1, 0), ("zs", 1, 1), ("pick", 0, 4), ("relay", 0, 5),
    ("score", 0, 3), ("ze", 1, 0, 0), ("relay", 0, 4), ("pick", 1, 0), ("ze", 1, 1, 0), ("score", 0, 5),
    ("ze", 1, 0, 1), ("pick", 1, 1), ("ze", 1, 1, 1), ("pick", 1, 7), ("relay", 1, 0), ("score", 0, 4), ("share", 0),
    ("partial", 0), ("ze", 1, 0, 2), ("ze", 1, 1, 2), ("relay", 1, 1), ("relay", 1, 7), ("whole", 0), ("ze", 1, 0, 3),
    ("ze", 1, 1, 3), ("pick", 1, 2), ("pick", 1, 6), ("weigh", 0), ("rf", 0), ("rf", 1), ("rf", 2), ("rf", 3),
    ("ro", 0), ("ze", 1, 0, 4), ("ze", 1, 1, 4), ("rc", 0), ("ro", 1), ("relay", 1, 2), ("rc", 1), ("ro", 2),
    ("rc", 2), ("ro", 3), ("rh", 0), ("rc", 3), ("rh", 1), ("rh", 2), ("ze", 1, 0, 5), ("pick", 1, 3), ("ze", 1, 1, 5),
    ("relay", 1, 6), ("pick", 1, 5), ("rh", 3), ("ze", 1, 0, 6), ("relay", 1, 3), ("ze", 1, 1, 6), ("pick", 1, 4),
    ("update",), ("relay", 1, 5), ("gather1",), ("gather2",), ("gather3",), ("score", 1, 0), ("relay", 1, 4),
    ("score", 1, 1), ("score", 1, 7), ("score", 1, 2), ("score", 1, 6), ("score", 1, 3), ("score", 1, 5),
    ("score", 1, 4), ("share", 1), ("partial", 1), ("whole", 1), ("weigh", 1), ("ls", 0), ("ls", 1), ("ls", 2),
    ("ls", 3), ("lq",), ("cnt",), ("lu",), ("own",), ("fin",),
)


def kernel(
    pts,
    cands,
    cent,
    out_sums,
    out_counts,
    zbufs,
    xs,
    outs,
    relays,
    tab,
    tab_in,
    tab_sm,
    scores,
    tops,
    w,
    lses,
    stats,
    sent_parts,
    parts_in,
    sent_shifts,
    shifts,
    psend,
    precv,
    phold,
    h1,
    h2,
    cur1,
    fb,
    fs,
    fr,
    g,
    q,
    u,
    cnts,
    z_send,
    z_recv,
    y_send,
    x_recv,
    r_recv,
    r_send,
    st_sem,
    tab_sem,
    dp_send,
    dp_recv,
    fin_send,
    fin_recv,
):
    dp = lax.axis_index("dp")
    cl = lax.axis_index("cluster")
    x, core = lax.div(dp, NC), lax.rem(dp, NC)
    z, y = lax.div(cl, NY), lax.rem(cl, NY)

    sign = 1 - 2 * core

    def at_cluster(k, dy):
        return {"cluster": lax.rem(z + sign * k + NZ, NZ) * NY + lax.rem(y + dy + NY, NY)}

    xp, xm, xo = lax.rem(x + 1, NX), lax.rem(x + 3, NX), lax.rem(x + 2, NX)
    dev_xp, dev_xm = {"dp": xp * NC + core}, {"dp": xm * NC + core}
    dev_core = {"dp": x * NC + 1 - core}
    z_devs = at_cluster(1, 0), at_cluster(-1, 0)
    y_up, y_down = at_cluster(0, 1), at_cluster(0, -1)

    barrier = pltpu.get_barrier_semaphore()
    for peer in [at_cluster(k, 0) for k in range(1, NZ)] + [at_cluster(0, p) for p in range(1, NY)]:
        pl.semaphore_signal(barrier, inc=1, device_id=peer, device_id_type=MESH)
    for j in range(1, NX * NC):
        pl.semaphore_signal(
            barrier, inc=1, device_id={"dp": lax.rem(dp + j, NX * NC)}, device_id_type=MESH
        )
    pl.semaphore_wait(barrier, NZ - 1 + NY - 1 + NX * NC - 1)

    drains = []

    def send(src, dst, ssem, rsem, dev):
        copy = pltpu.make_async_remote_copy(
            src_ref=src,
            dst_ref=dst,
            send_sem=ssem,
            recv_sem=rsem,
            device_id=dev,
            device_id_type=MESH,
        )
        copy.start()
        return copy

    def landed(ref, sem):
        pltpu.make_async_copy(ref, ref, sem).wait()

    def later(ref, sem):
        drains.append(lambda: landed(ref, sem))

    def drain():
        for wait in drains:
            wait()
        drains.clear()

    def half(ref, h):
        return ref.at[pl.ds(h * 4, 4)]

    def chunk(step, k):
        return pts.at[step] if k == 0 else zbufs[step * 7 + k - 1]

    def z_start(step, d):
        order = (PLUS, MINUS)[d]
        for i in range(2):
            k, h = order[i]
            src = half(pts.at[step], h)
            dst = half(chunk(step, k), h)
            send(src, dst, z_send.at[step, d, i], z_recv.at[step, d, i], z_devs[d])
            later(src, z_send.at[step, d, i])

    def z_event(step, d, i):
        order = (PLUS, MINUS)[d]
        k, h = order[i]
        here = half(chunk(step, k), h)
        landed(here, z_recv.at[step, d, i])
        if i < 5:
            dst = half(chunk(step, order[i + 2][0]), h)
            send(here, dst, z_send.at[step, d, i + 2], z_recv.at[step, d, i + 2], z_devs[d])
            later(here, z_send.at[step, d, i + 2])

    def tables():
        row = lax.broadcasted_iota(jnp.int32, (8, 128), 0)
        lane = lax.broadcasted_iota(jnp.int32, (8, 128), 1)
        oz = (z + sign * row) & (NZ - 1)
        second = ((lane >> 5) & 1) == 1
        for step in range(2):
            for t in range(2):
                owner = oz * NY + ((y + t * 2 + (lane >> 6)) & (NY - 1))
                first = jnp.full((8, 128), NB, jnp.int32)
                last = jnp.full((8, 128), -1, jnp.int32)
                for b in range(NB):
                    hit = owner == cands[step, b, 0]
                    for j in range(1, 4):
                        hit = hit | (owner == cands[step, b, j])
                    last = jnp.where(hit, b, last)
                    first = jnp.minimum(first, jnp.where(hit, b, NB))
                lone = jnp.where(first < NB, first, -1)
                bid = jnp.where(second, jnp.where(last > first, last, -1), lone)
                off = step * 256 + t * 128
                tab[:, :, off : off + 128] = bid.reshape(8, 1, 128)
        for k in range(1, NZ):
            send(tab.at[k], tab_in.at[k], tab_sem.at[0], tab_sem.at[1], at_cluster(k, 0))
        later(tab_in.at[pl.ds(1, 7)], tab_sem.at[0])
        tab_in[0] = tab[0]
        to_scalars(tab, 0, 1)

    def to_scalars(table, first, count):
        rows = pl.ds(first, count)
        copy = pltpu.make_async_copy(table.at[rows], tab_sm.at[rows], tab_sem.at[2])
        copy.start()
        copy.wait()

    def tables_in():
        landed(tab_in.at[pl.ds(1, 7)], tab_sem.at[1])
        to_scalars(tab_in, 1, 7)

    def pick(step, k):
        source, xr, box = chunk(step, k), xs[step], outs[step]

        def block(p, s):
            number = tab_sm[k, 0, step * 256 + p * 64 + s * 32]
            return source[jnp.maximum(number, 0)]

        sems = (y_send.at[step, k], x_recv.at[step, k])
        box[k, 2] = block(2, 0)
        send(box.at[k, 2], relays[step].at[k, 0], sems[0], r_recv.at[step, k, 0], y_up)
        box[k, 3] = block(2, 1)
        send(box.at[k, 3], relays[step].at[k, 1], sems[0], r_recv.at[step, k, 1], y_down)
        for p, dev in ((1, y_up), (3, y_down)):
            first = 0 if p == 1 else 4
            box[k, first] = block(p, 0)
            box[k, first + 1] = block(p, 1)
            send(
                box.at[k, pl.ds(first, 2)], xr.at[pl.ds(k * 8 + p * 2, 2)], sems[0], sems[1], dev
            )
        later(box.at[k], sems[0])
        xr[k * 8] = block(0, 0)
        xr[k * 8 + 1] = block(0, 1)

    def relay(step, k):
        for s, dev in enumerate((y_up, y_down)):
            here = relays[step].at[k, s]
            landed(here, r_recv.at[step, k, s])
            send(
                here,
                xs[step].at[k * 8 + 4 + s],
                r_send.at[step, k],
                x_recv.at[step, k],
                dev,
            )
        later(relays[step].at[k], r_send.at[step, k])

    def score(step, k):
        xr, centroids = xs[step], (cent, cur1)[step]
        landed(xr.at[pl.ds(k * 8 + 2, 6)], x_recv.at[step, k])
        rows = xr[k * 8 : k * 8 + 8].reshape(8 * PB, D)
        s = lax.dot_general(
            centroids[...], rows, (((1,), (1,)), ((), ())), preferred_element_type=F32
        )
        top = jnp.max(s, axis=0, keepdims=True)
        e = jnp.exp(s - top)
        scores[k] = e
        tops[k] = top
        total = jnp.sum(e, axis=0, keepdims=True)
        lse = top + jnp.log(total)
        for i in range(2):
            lses[step][i, k : k + 1, :] = lse[:, i * 128 : (i + 1) * 128]

    low = lax.broadcasted_iota(jnp.int32, (1, 128), 1) < 64
    group = lax.broadcasted_iota(jnp.int32, (1, 128), 1) >> 5

    def over_groups(op, value):
        value = op(value, pltpu.roll(value, 64, 1))
        return op(value, pltpu.roll(value, 32, 1))

    def block_ids(step):
        return [
            tab_in[:, :, step * 256 + i * 128 : step * 256 + i * 128 + 128].reshape(8, 128)
            for i in range(2)
        ]

    def share(step):
        for p in range(1, NY):
            send(
                lses[step].at[p >> 1],
                stats[step].at[p],
                st_sem.at[step, 0],
                st_sem.at[step, 1],
                at_cluster(0, -p),
            )
        stats[step][0] = lses[step][0]
        later(stats[step].at[pl.ds(1, 3)], st_sem.at[step, 0])

    def partial(step):
        got = stats[step]
        landed(got.at[pl.ds(1, 3)], st_sem.at[step, 1])
        have = [jnp.where(low, got[2 * i], got[2 * i + 1]) for i in range(2)]
        ids = block_ids(step)
        packed = [jnp.full((8, 128), -BIG, F32) for _ in range(2)]
        for b in range(NB):
            mine = [ids[i] == b for i in range(2)]
            masked = [jnp.where(mine[i], have[i], -BIG) for i in range(2)]
            top = over_groups(jnp.maximum, jnp.maximum(masked[0], masked[1]))
            each = [jnp.where(mine[i], jnp.exp(have[i] - top), 0.0) for i in range(2)]
            total = over_groups(jnp.add, each[0] + each[1])
            value = jnp.where(total > 0.0, top + jnp.log(total), -BIG)
            packed[b >> 2] = jnp.where(group == (b & 3), value, packed[b >> 2])
        out = sent_parts[step]
        for i in range(2):
            out[i * 8 : i * 8 + 8, :] = packed[i]
        for j in range(1, NZ):
            send(
                out,
                parts_in[step].at[j],
                st_sem.at[step, 2],
                st_sem.at[step, 3],
                at_cluster(j, 0),
            )
        later(parts_in[step].at[pl.ds(1, 7)], st_sem.at[step, 2])

    def whole(step):
        into = parts_in[step]
        landed(into.at[pl.ds(1, 7)], st_sem.at[step, 3])
        ids = block_ids(step)
        shift = [jnp.full((8, 128), BIG, F32) for _ in range(2)]
        for i in range(2):
            rows = slice(i * 8, i * 8 + 8)
            seen = [sent_parts[step][rows, :]]
            for j in range(1, NZ):
                seen.append(pltpu.roll(into[j, rows, :], j, 0))
            top = seen[0]
            for j in range(1, NZ):
                top = jnp.maximum(top, seen[j])
            total = jnp.exp(seen[0] - top)
            for j in range(1, NZ):
                total = total + jnp.exp(seen[j] - top)
            value = top + jnp.log(total)
            for b in range(4):
                spread = over_groups(jnp.maximum, jnp.where(group == b, value, -BIG))
                for t in range(2):
                    shift[t] = jnp.where(ids[t] == i * 4 + b, spread, shift[t])
        out, back = sent_shifts[step], shifts[step]
        for t in range(2):
            out[t] = shift[t]
        back[0] = shift[0]
        for p in range(1, NY):
            send(
                out.at[p >> 1],
                back.at[p],
                st_sem.at[step, 4],
                st_sem.at[step, 5],
                at_cluster(0, p),
            )
        later(back.at[pl.ds(1, 3)], st_sem.at[step, 4])

    def weigh(step):
        back = shifts[step]
        landed(back.at[pl.ds(1, 3)], st_sem.at[step, 5])
        for k in range(NZ):
            for t in range(2):
                shift = jnp.where(low, back[2 * t, k : k + 1, :], back[2 * t + 1, k : k + 1, :])
                lanes = pl.ds(k * 256 + t * 128, 128)
                scale = jnp.exp(tops[k, :, t * 128 : (t + 1) * 128] - shift)
                w[:, lanes] = (scores[k, :, t * 128 : (t + 1) * 128] * scale).astype(BF16)

    def half_sums(which, n):
        rows = w[pl.ds(pl.multiple_of(which * 256, 256), 256), :]
        cols = xs[0][:, :, n * 256 : (n + 1) * 256].reshape(64 * PB, 256)
        return jnp.dot(rows, cols, preferred_element_type=F32)

    def rows64(at, count=64, shift=0):
        return pl.ds(pl.multiple_of(at * 64 + shift, 32), count)

    def rf(n):
        psend[n] = half_sums(1 - core, n)
        send(psend.at[n], precv.at[n], dp_send.at[n], dp_recv.at[n], dev_core)
        later(psend.at[n], dp_send.at[n])

    def ro(n):
        phold[n] = half_sums(core, n)

    def rc(n):
        landed(precv.at[n], dp_recv.at[n])
        far = rows64(xo)
        phold[n, far, :] = phold[n, far, :] + precv[n, far, :]
        sides = ((rows64(xo, 32), dev_xp), (rows64(xo, 32, 32), dev_xm))
        for i, (part, dev) in enumerate(sides):
            sems = dp_send.at[4 + 4 * i + n], dp_recv.at[4 + 4 * i + n]
            send(phold.at[n, part, :], h1.at[i, n], sems[0], sems[1], dev)
            later(h1.at[i, n], sems[0])
        for at in (xp, xm, x):
            near = rows64(at)
            phold[n, near, :] = phold[n, near, :] + precv[n, near, :]

    def rh(n):
        sides = ((xp, 0, dev_xp), (xm, 32, dev_xm))
        for i, (at, shift, dev) in enumerate(sides):
            landed(h1.at[i, n], dp_recv.at[4 + 4 * i + n])
            part = rows64(at, 32, shift)
            phold[n, part, :] = phold[n, part, :] + h1[i, n]
            sems = dp_send.at[12 + 4 * i + n], dp_recv.at[12 + 4 * i + n]
            send(phold.at[n, rows64(at), :], h2.at[i, n], sems[0], sems[1], dev)
            later(h2.at[i, n], sems[0])

    def cur_rows(which_core, at, count=64, shift=0):
        return pl.ds(pl.multiple_of(which_core * 256 + at * 64 + shift, 32), count)

    def update():
        for n in range(4):
            landed(h2.at[0, n], dp_recv.at[12 + n])
            landed(h2.at[1, n], dp_recv.at[16 + n])
        own = rows64(x)
        mine = cur_rows(core, x)
        v = [
            cent[mine, n * 256 : (n + 1) * 256].astype(F32)
            + (phold[n, own, :] + h2[0, n] + h2[1, n])
            for n in range(4)
        ]
        square = sum(jnp.sum(part * part, axis=1, keepdims=True) for part in v)
        norm = jnp.sqrt(square + 1e-06)
        for n in range(4):
            cur1[mine, n * 256 : (n + 1) * 256] = (v[n] / norm).astype(BF16)
        here = cur1.at[mine]
        send(here, here, dp_send.at[20], dp_recv.at[20], dev_xp)
        send(here, here, dp_send.at[21], dp_recv.at[21], dev_xm)
        send(here, here, dp_send.at[22], dp_recv.at[24], dev_core)
        for i in (20, 21, 22):
            later(here, dp_send.at[i])

    def gather1():
        sides = ((xm, 0, dev_xp), (xp, 32, dev_xm))
        for i, (at, shift, dev) in enumerate(sides):
            here = cur1.at[cur_rows(core, at)]
            landed(here, dp_recv.at[20 + i])
            part = cur1.at[cur_rows(core, at, 32, shift)]
            send(part, part, dp_send.at[23 + i], dp_recv.at[22 + i], dev)
            later(part, dp_send.at[23 + i])
            send(here, here, dp_send.at[25 + i], dp_recv.at[24], dev_core)
            later(here, dp_send.at[25 + i])

    def gather2():
        for i, shift in enumerate((0, 32)):
            part = cur1.at[cur_rows(core, xo, 32, shift)]
            landed(part, dp_recv.at[22 + i])
            send(part, part, dp_send.at[27 + i], dp_recv.at[24], dev_core)
            later(part, dp_send.at[27 + i])

    def gather3():
        other = pl.ds(pl.multiple_of((1 - core) * 256, 256), 256)
        landed(cur1.at[other], dp_recv.at[24])

    def ls(j):
        lanes = pl.ds(pl.multiple_of((xo, xp, xm, x)[j] * 256, 256), 256)
        cols = xs[1][:, :, lanes].reshape(64 * PB, 256)
        part = jnp.dot(w[...], cols, preferred_element_type=F32)
        fb[j, 0] = part[:, :128]
        fb[j, 1] = part[:, 128:]
        fs[j] = fb[j, 1 - core].astype(BF16)
        send(fs.at[j], fr.at[j], fin_send.at[0], fin_recv.at[j], dev_core)
        if j == 3:
            later(fs, fin_send.at[0])

    def both(j):
        landed(fr.at[j], fin_recv.at[j])
        return fb[j, core] + fr[j].astype(F32)

    def lq():
        g[0] = both(0).astype(BF16)
        for i, dev in enumerate((dev_xp, dev_xm)):
            rows = pl.ds(256 * i, 256)
            send(g.at[0, rows], q.at[i], fin_send.at[2 + i], fin_recv.at[5 + i], dev)
            later(q.at[i], fin_send.at[2 + i])

    def lu():
        for i, dev in enumerate((dev_xp, dev_xm)):
            part = both(1 + i)
            landed(q.at[i], fin_recv.at[5 + i])
            with_q, rest = pl.ds(256 * i, 256), pl.ds(256 - 256 * i, 256)
            parts = part[:256], part[256:]
            g[1 + i, rest] = parts[1 - i].astype(BF16)
            g[1 + i, with_q] = (parts[i] + q[i].astype(F32)).astype(BF16)
            send(g.at[1 + i], u.at[i], fin_send.at[4 + i], fin_recv.at[7 + i], dev)
            later(u.at[i], fin_send.at[4 + i])

    def cnt():
        ones = jnp.ones((8, 64 * PB), BF16)
        count = lax.dot_general(
            ones, w[...], (((1,), (1,)), ((), ())), preferred_element_type=F32
        )
        cnts[dp] = count[0:1]
        for j in range(1, NX * NC):
            send(
                cnts.at[dp],
                cnts.at[dp],
                fin_send.at[1],
                fin_recv.at[4],
                {"dp": lax.rem(dp + j, NX * NC)},
            )
        later(cnts.at[pl.ds(0, 7)], fin_send.at[1])

    def own():
        fb[3, core] = both(3)
        landed(cnts.at[pl.ds(0, 7)], fin_recv.at[4])
        count = cnts[0]
        for j in range(1, NX * NC):
            count = count + cnts[j]
        for j in range(4):
            out_counts[j : j + 1, :] = count[:, j * 128 : (j + 1) * 128]
        drain()

    def fin():
        landed(u.at[0], fin_recv.at[7])
        landed(u.at[1], fin_recv.at[8])
        out_sums[...] = fb[3, core] + (u[0].astype(F32) + u[1].astype(F32))

    parts = dict(
        zs=z_start,
        ze=z_event,
        pick=pick,
        relay=relay,
        score=score,
        share=share,
        partial=partial,
        whole=whole,
        weigh=weigh,
        rf=rf,
        ro=ro,
        rc=rc,
        rh=rh,
        update=update,
        gather1=gather1,
        gather2=gather2,
        gather3=gather3,
        ls=ls,
        lq=lq,
        lu=lu,
        cnt=cnt,
        own=own,
        fin=fin,
    )
    for name, *numbers in SCHEDULE:
        parts[name](*numbers)
        if (name, *numbers) == ("zs", 0, 0):
            tables()
        if (name, *numbers) == ("relay", 0, 0):
            tables_in()


def on_device(points, candidates, centroids):
    vmem = pl.BlockSpec(memory_space=pltpu.VMEM)
    sem = pltpu.SemaphoreType.DMA
    steps = points.shape[0]
    sums, counts = pl.pallas_call(
        kernel,
        out_shape=(
            jax.ShapeDtypeStruct((CBS, D // (NX * NC)), F32),
            jax.ShapeDtypeStruct((4, 128), F32),
        ),
        in_specs=[vmem, pl.BlockSpec(memory_space=pltpu.SMEM), vmem],
        out_specs=(vmem, vmem),
        scratch_shapes=[
            [pltpu.VMEM((NB, PB, D), BF16) for _ in range(7 * steps)],
            [pltpu.VMEM((64, PB, D), BF16) for _ in range(steps)],
            [pltpu.VMEM((NZ, 6, PB, D), BF16) for _ in range(steps)],
            [pltpu.VMEM((NZ, 2, PB, D), BF16) for _ in range(steps)],
            pltpu.VMEM((NZ, 1, 512), jnp.int32),
            pltpu.VMEM((NZ, 1, 512), jnp.int32),
            pltpu.SMEM((NZ, 1, 512), jnp.int32),
            pltpu.VMEM((NZ, CBS, 256), F32),
            pltpu.VMEM((NZ, 1, 256), F32),
            pltpu.VMEM((CBS, 64 * PB), BF16),
            [pltpu.VMEM((2, 8, 128), F32) for _ in range(steps)],
            [pltpu.VMEM((4, 8, 128), F32) for _ in range(steps)],
            [pltpu.VMEM((16, 128), F32) for _ in range(steps)],
            [pltpu.VMEM((NZ, 16, 128), F32) for _ in range(steps)],
            [pltpu.VMEM((2, 8, 128), F32) for _ in range(steps)],
            [pltpu.VMEM((4, 8, 128), F32) for _ in range(steps)],
            pltpu.VMEM((4, 256, 256), F32),
            pltpu.VMEM((4, 256, 256), F32),
            pltpu.VMEM((4, 256, 256), F32),
            pltpu.VMEM((2, 4, 32, 256), F32),
            pltpu.VMEM((2, 4, 64, 256), F32),
            pltpu.VMEM((CBS, D), BF16),
            pltpu.VMEM((4, 2, CBS, 128), F32),
            pltpu.VMEM((4, CBS, 128), BF16),
            pltpu.VMEM((4, CBS, 128), BF16),
            pltpu.VMEM((3, CBS, 128), BF16),
            pltpu.VMEM((2, 256, 128), BF16),
            pltpu.VMEM((2, CBS, 128), BF16),
            pltpu.VMEM((NX * NC, 1, CBS), F32),
            sem((steps, 2, 7)),
            sem((steps, 2, 7)),
            sem((steps, NZ)),
            sem((steps, NZ)),
            sem((steps, NZ, 2)),
            sem((steps, NZ)),
            sem((steps, 6)),
            sem((3,)),
            sem((29,)),
            sem((25,)),
            sem((6,)),
            sem((9,)),
        ],
        compiler_params=pltpu.CompilerParams(
            collective_id=0, has_side_effects=True, vmem_limit_bytes=56 * 1024 * 1024
        ),
    )(points.reshape(steps, NB, PB, D), candidates, centroids)
    return sums, counts.reshape(CBS)


def solution(mesh):
    placed = (
        P(None, ("dp", "cluster"), None),
        P(None, ("dp", "cluster"), None),
        P("cluster", None),
    )
    return jax.shard_map(
        on_device,
        mesh=mesh,
        in_specs=placed,
        out_specs=(P("cluster", "dp"), P("cluster")),
        check_vma=False,
    )
```

time: 396 us -> 156 us (0.39)
  waiting for transfers between devices: 250 us -> 0 us
  Pallas kernels: 0 us -> 152 us
  starting transfers between devices: 53.1 us -> 0 us
  matrix products: 31.4 us -> 0 us
  local copies, waits for them, and re-layouts: 20 us -> 3.62 us
  between operations: 14.3 us -> 0.65 us
  other arithmetic: 11.8 us -> 0 us
  blocking collectives: 11 us -> 0 us
    all_to_all x10 -> x0, waiting for transfers between devices: 167 us -> none  [the longest x2 106 us: on_device(): lax.all_to_all(message, 'cluster', split_axis=0, concat_axis=0, tiled=True)]
    pallas_call x0 -> x1, Pallas kernels: none -> 152 us  [on_device(): pl.pallas_call(kernel, out_shape=(jax.ShapeDtypeStruct((CBS, D // (NX * N...]
    psum x1 -> x0, waiting for transfers between devices: 70.9 us -> none  [on_device(): summed = lax.psum(block_sums, 'dp')]
    all_to_all x10 -> x0, starting transfers between devices: 52.7 us -> none  [the longest x2 17.6 us: on_device(): lax.all_to_all(message, 'cluster', split_axis=0, concat_axis=0, tiled=True)]
    dot_general x16 -> x0, matrix products: 31.4 us -> none  [the longest x2 13.8 us: score_rows(): jnp.einsum('rd,cd->rc', arrived_rows, centroid_rows, preferred_element_ty...]
    unnamed x3 -> x0, waiting for transfers between devices: 12.1 us -> none
    psum x1 -> x0, blocking collectives: 11 us -> none  [on_device(): final_counts = lax.psum(block_counts, 'dp')]
    reduce_sum x6 -> x0, other arithmetic: 10.8 us -> none  [the longest x2 5.56 us: owner_sums(): row_total = jnp.sum(jnp.exp(scores - row_max[:, None]), axis=1)]
  transfers between devices with their start and end apart: 12 -> 0, of which waited for: 12 -> 0; matrix products, arithmetic and copies ran while one was open for 7% -> 0% of each run, Pallas kernels for 0% -> 0%
where the time goes in v1:
time: 156 us
  Pallas kernels  152 us (97%)
  local copies, waits for them, and re-layouts  3.62 us (2%)
    pallas_call x1, Pallas kernels, on_device(): pl.pallas_call(kernel, out_shape=(jax.ShapeDtypeStruct((CBS, D // (NX * N...  152 us
    unnamed x5, local copies, waits for them, and re-layouts  3.62 us

profile of v1, /device:TPU:2, one launch (start us, length us, event | category | flops | bytes accessed | tf_op | source)
XLA Modules:
  0.0 155.9 jit_solution(5782530144490731143)
XLA Ops:
  0.6 1.4 copy.5.cands
  2.0 151.6 %shard_map.50 = (f32[512,128]{1,0:T(8,128)}, f32[4,128]{1,0:T(4,128)}) custom-call(bf16[2,8,32,1024]{3,2,1,0:T(8,128)(2,1)} %bitcast.2, s32[2,8,4]{2,1,0:T(8,128)} %copy.5.cands, bf16[512,1024]{1,0:T(8,128)(2,1)} %cent.1), custom_call_target="tpu_custom_call" | custom-call | tf_op jit(solution)/shard_map/pallas_call | solution.py:532
  153.6 0.0 copy-start
  153.7 1.7 %copy.8 = f32[512,128]{1,0:T(8,128)} copy(f32[512,128]{1,0:T(8,128)} %get-tuple-element.8) | data formatting | bytes 524288
  155.3 0.0 copy-done
  155.3 0.6 copy.9
Async XLA Ops:
  153.6 1.7 %copy-start = (f32[4,128]{1,0:T(4,128)S(1)}, f32[4,128]{1,0:T(4,128)}, u32[]{:S(2)}) copy-start(f32[4,128]{1,0:T(4,128)} %get-tuple-element.5) | copy-start | bytes 6148

commit v2 on v1

--- a/solution.py
+++ b/solution.py
@@ -14,32 +14,34 @@
 PLUS = ((1, 0), (1, 1), (2, 0), (2, 1), (3, 0), (3, 1), (4, 0))
 MINUS = ((7, 1), (7, 0), (6, 1), (6, 0), (5, 1), (5, 0), (4, 1))
 SCHEDULE = (
-    ("zs", 0, 0), ("zs", 0, 1), ("pick", 0, 0), ("relay", 0, 0), ("ze", 0, 0, 0), ("ze", 0, 1, 0), ("score", 0, 0),
-    ("ze", 0, 0, 1), ("pick", 0, 1), ("ze", 0, 1, 1), ("pick", 0, 7), ("relay", 0, 1), ("ze", 0, 0, 2),
-    ("ze", 0, 1, 2), ("relay", 0, 7), ("ze", 0, 0, 3), ("pick", 0, 2), ("ze", 0, 1, 3), ("pick", 0, 6),
-    ("score", 0, 1), ("score", 0, 7), ("relay", 0, 2), ("ze", 0, 0, 4), ("ze", 0, 1, 4), ("relay", 0, 6),
-    ("ze", 0, 0, 5), ("pick", 0, 3), ("ze", 0, 1, 5), ("pick", 0, 5), ("score", 0, 2), ("score", 0, 6),
-    ("relay", 0, 3), ("ze", 0, 0, 6), ("ze", 0, 1, 6), ("zs", 1, 0), ("zs", 1, 1), ("pick", 0, 4), ("relay", 0, 5),
-    ("score", 0, 3), ("ze", 1, 0, 0), ("relay", 0, 4), ("pick", 1, 0), ("ze", 1, 1, 0), ("score", 0, 5),
-    ("ze", 1, 0, 1), ("pick", 1, 1), ("ze", 1, 1, 1), ("pick", 1, 7), ("relay", 1, 0), ("score", 0, 4), ("share", 0),
-    ("partial", 0), ("ze", 1, 0, 2), ("ze", 1, 1, 2), ("relay", 1, 1), ("relay", 1, 7), ("whole", 0), ("ze", 1, 0, 3),
-    ("ze", 1, 1, 3), ("pick", 1, 2), ("pick", 1, 6), ("weigh", 0), ("rf", 0), ("rf", 1), ("rf", 2), ("rf", 3),
-    ("ro", 0), ("ze", 1, 0, 4), ("ze", 1, 1, 4), ("rc", 0), ("ro", 1), ("relay", 1, 2), ("rc", 1), ("ro", 2),
-    ("rc", 2), ("ro", 3), ("rh", 0), ("rc", 3), ("rh", 1), ("rh", 2), ("ze", 1, 0, 5), ("pick", 1, 3), ("ze", 1, 1, 5),
-    ("relay", 1, 6), ("pick", 1, 5), ("rh", 3), ("ze", 1, 0, 6), ("relay", 1, 3), ("ze", 1, 1, 6), ("pick", 1, 4),
-    ("update",), ("relay", 1, 5), ("gather1",), ("gather2",), ("gather3",), ("score", 1, 0), ("relay", 1, 4),
-    ("score", 1, 1), ("score", 1, 7), ("score", 1, 2), ("score", 1, 6), ("score", 1, 3), ("score", 1, 5),
-    ("score", 1, 4), ("share", 1), ("partial", 1), ("whole", 1), ("weigh", 1), ("ls", 0), ("ls", 1), ("ls", 2),
-    ("ls", 3), ("lq",), ("cnt",), ("lu",), ("own",), ("fin",),
+    ("zs", 0, 0), ("zs", 0, 1), ("pick", 0, 0), ("pick", 1, 0), ("relay", 0, 0), ("ze", 0, 0, 0), ("ze", 0, 1, 0),
+    ("relay", 1, 0), ("score", 0, 0), ("ze", 0, 0, 1), ("ze", 0, 1, 1), ("pick", 0, 1), ("pick", 0, 7),
+    ("relay", 0, 1), ("ze", 0, 0, 2), ("ze", 0, 1, 2), ("relay", 0, 7), ("ze", 0, 0, 3), ("pick", 0, 2),
+    ("ze", 0, 1, 3), ("pick", 0, 6), ("score", 0, 1), ("score", 0, 7), ("relay", 0, 2), ("ze", 0, 0, 4),
+    ("ze", 0, 1, 4), ("relay", 0, 6), ("ze", 0, 0, 5), ("pick", 0, 3), ("ze", 0, 1, 5), ("pick", 0, 5),
+    ("score", 0, 2), ("score", 0, 6), ("relay", 0, 3), ("ze", 0, 0, 6), ("ze", 0, 1, 6), ("zs", 1, 0), ("zs", 1, 1),
+    ("pick", 0, 4), ("relay", 0, 5), ("ze", 1, 0, 0), ("ze", 1, 1, 0), ("score", 0, 3), ("relay", 0, 4),
+    ("ze", 1, 0, 1), ("pick", 1, 1), ("ze", 1, 1, 1), ("pick", 1, 7), ("score", 0, 5), ("score", 0, 4), ("share", 0),
+    ("relay", 1, 1), ("partial", 0), ("ze", 1, 0, 2), ("ze", 1, 1, 2), ("relay", 1, 7), ("whole", 0), ("ze", 1, 0, 3),
+    ("pick", 1, 2), ("ze", 1, 1, 3), ("pick", 1, 6), ("weigh", 0), ("rf", 0), ("ro", 0), ("rf", 1), ("ro", 1),
+    ("relay", 1, 2), ("rc", 0), ("rf", 2), ("rc", 1), ("ze", 1, 0, 4), ("ze", 1, 1, 4), ("ro", 2), ("rh", 0),
+    ("rf", 3), ("rc", 2), ("rh", 1), ("relay", 1, 6), ("ro", 3), ("rc", 3), ("rh", 2), ("ze", 1, 0, 5), ("pick", 1, 3),
+    ("ze", 1, 1, 5), ("pick", 1, 5), ("rh", 3), ("update",), ("relay", 1, 3), ("ze", 1, 0, 6), ("ze", 1, 1, 6),
+    ("pick", 1, 4), ("gather1",), ("gather1b",), ("relay", 1, 5), ("gather2",), ("gather3",), ("score", 1, 0),
+    ("score", 1, 1), ("score", 1, 7), ("score", 1, 2), ("relay", 1, 4), ("score", 1, 6), ("score", 1, 3),
+    ("score", 1, 5), ("score", 1, 4), ("share", 1), ("partial", 1), ("whole", 1), ("weigh", 1), ("ls", 0), ("ls", 1),
+    ("ls", 2), ("lq",), ("ls", 3), ("cnt",), ("lv",), ("lu",), ("own",), ("fin",),
 )
 
 
 def kernel(
-    pts,
+    pts_hbm,
     cands,
-    cent,
+    cent_hbm,
     out_sums,
     out_counts,
+    pts,
+    cent,
     zbufs,
     xs,
     outs,
@@ -81,6 +83,7 @@
     dp_recv,
     fin_send,
     fin_recv,
+    load_sem,
 ):
     dp = lax.axis_index("dp")
     cl = lax.axis_index("cluster")
@@ -97,6 +100,13 @@
     dev_core = {"dp": x * NC + 1 - core}
     z_devs = at_cluster(1, 0), at_cluster(-1, 0)
     y_up, y_down = at_cluster(0, 1), at_cluster(0, -1)
+
+    loads = [
+        pltpu.make_async_copy(pts_hbm, pts, load_sem.at[0]),
+        pltpu.make_async_copy(cent_hbm, cent, load_sem.at[1]),
+    ]
+    for load in loads:
+        load.start()
 
     barrier = pltpu.get_barrier_semaphore()
     for peer in [at_cluster(k, 0) for k in range(1, NZ)] + [at_cluster(0, p) for p in range(1, NY)]:
@@ -121,6 +131,12 @@
         copy.start()
         return copy
 
+    def send_cut(src, dst, ssem, rsem, dev):
+        size = src.shape[0] // 2
+        for i in range(2):
+            part = pl.ds(i * size, size)
+            send(src.at[part], dst.at[part], ssem, rsem, dev)
+
     def landed(ref, sem):
         pltpu.make_async_copy(ref, ref, sem).wait()
 
@@ -142,9 +158,9 @@
         order = (PLUS, MINUS)[d]
         for i in range(2):
             k, h = order[i]
-            src = half(pts.at[step], h)
+            src = half(pts_hbm.at[step], h)
             dst = half(chunk(step, k), h)
-            send(src, dst, z_send.at[step, d, i], z_recv.at[step, d, i], z_devs[d])
+            send_cut(src, dst, z_send.at[step, d, i], z_recv.at[step, d, i], z_devs[d])
             later(src, z_send.at[step, d, i])
 
     def z_event(step, d, i):
@@ -154,7 +170,7 @@
         landed(here, z_recv.at[step, d, i])
         if i < 5:
             dst = half(chunk(step, order[i + 2][0]), h)
-            send(here, dst, z_send.at[step, d, i + 2], z_recv.at[step, d, i + 2], z_devs[d])
+            send_cut(here, dst, z_send.at[step, d, i + 2], z_recv.at[step, d, i + 2], z_devs[d])
             later(here, z_send.at[step, d, i + 2])
 
     def tables():
@@ -168,9 +184,9 @@
                 first = jnp.full((8, 128), NB, jnp.int32)
                 last = jnp.full((8, 128), -1, jnp.int32)
                 for b in range(NB):
-                    hit = owner == cands[step, b, 0]
+                    hit = owner == cands[step, 0, b]
                     for j in range(1, 4):
-                        hit = hit | (owner == cands[step, b, j])
+                        hit = hit | (owner == cands[step, j, b])
                     last = jnp.where(hit, b, last)
                     first = jnp.minimum(first, jnp.where(hit, b, NB))
                 lone = jnp.where(first < NB, first, -1)
@@ -209,7 +225,7 @@
             first = 0 if p == 1 else 4
             box[k, first] = block(p, 0)
             box[k, first + 1] = block(p, 1)
-            send(
+            send_cut(
                 box.at[k, pl.ds(first, 2)], xr.at[pl.ds(k * 8 + p * 2, 2)], sems[0], sems[1], dev
             )
         later(box.at[k], sems[0])
@@ -370,16 +386,21 @@
         for at in (xp, xm, x):
             near = rows64(at)
             phold[n, near, :] = phold[n, near, :] + precv[n, near, :]
+        for i, (at, shift, dev) in enumerate(((xp, 32, dev_xp), (xm, 0, dev_xm))):
+            second_hop(n, i, at, shift, dev)
+
+    def second_hop(n, i, at, shift, dev):
+        sems = dp_send.at[12 + 4 * i + n], dp_recv.at[12 + 4 * i + n]
+        src = phold.at[n, rows64(at, 32, shift), :]
+        send(src, h2.at[i, n, pl.ds(shift, 32)], sems[0], sems[1], dev)
 
     def rh(n):
-        sides = ((xp, 0, dev_xp), (xm, 32, dev_xm))
-        for i, (at, shift, dev) in enumerate(sides):
+        for i, (at, shift, dev) in enumerate(((xp, 0, dev_xp), (xm, 32, dev_xm))):
             landed(h1.at[i, n], dp_recv.at[4 + 4 * i + n])
             part = rows64(at, 32, shift)
             phold[n, part, :] = phold[n, part, :] + h1[i, n]
-            sems = dp_send.at[12 + 4 * i + n], dp_recv.at[12 + 4 * i + n]
-            send(phold.at[n, rows64(at), :], h2.at[i, n], sems[0], sems[1], dev)
-            later(h2.at[i, n], sems[0])
+            second_hop(n, i, at, shift, dev)
+            later(h2.at[i, n], dp_send.at[12 + 4 * i + n])
 
     def cur_rows(which_core, at, count=64, shift=0):
         return pl.ds(pl.multiple_of(which_core * 256 + at * 64 + shift, 32), count)
@@ -399,34 +420,41 @@
         norm = jnp.sqrt(square + 1e-06)
         for n in range(4):
             cur1[mine, n * 256 : (n + 1) * 256] = (v[n] / norm).astype(BF16)
-        here = cur1.at[mine]
-        send(here, here, dp_send.at[20], dp_recv.at[20], dev_xp)
-        send(here, here, dp_send.at[21], dp_recv.at[21], dev_xm)
-        send(here, here, dp_send.at[22], dp_recv.at[24], dev_core)
-        for i in (20, 21, 22):
-            later(here, dp_send.at[i])
+        pieces = ((0, dev_xp, 20), (32, dev_xm, 21), (32, dev_xp, 22), (0, dev_xm, 23))
+        for i, (shift, dev, sem) in enumerate(pieces):
+            part = cur1.at[cur_rows(core, x, 32, shift)]
+            send(part, part, dp_send.at[sem], dp_recv.at[sem], dev)
+            later(part, dp_send.at[sem])
+            if i == 1:
+                to_core(cur1.at[mine], 24)
+
+    def to_core(part, sem):
+        send(part, part, dp_send.at[sem], dp_recv.at[26], dev_core)
+        later(part, dp_send.at[sem])
 
     def gather1():
-        sides = ((xm, 0, dev_xp), (xp, 32, dev_xm))
-        for i, (at, shift, dev) in enumerate(sides):
-            here = cur1.at[cur_rows(core, at)]
-            landed(here, dp_recv.at[20 + i])
+        for i, (at, shift, dev) in enumerate(((xm, 0, dev_xp), (xp, 32, dev_xm))):
             part = cur1.at[cur_rows(core, at, 32, shift)]
-            send(part, part, dp_send.at[23 + i], dp_recv.at[22 + i], dev)
-            later(part, dp_send.at[23 + i])
-            send(here, here, dp_send.at[25 + i], dp_recv.at[24], dev_core)
-            later(here, dp_send.at[25 + i])
+            landed(part, dp_recv.at[20 + i])
+            send(part, part, dp_send.at[25 + i], dp_recv.at[24 + i], dev)
+            later(part, dp_send.at[25 + i])
+            to_core(part, 27 + i)
+
+    def gather1b():
+        for i, (at, shift) in enumerate(((xm, 32), (xp, 0))):
+            part = cur1.at[cur_rows(core, at, 32, shift)]
+            landed(part, dp_recv.at[22 + i])
+            to_core(part, 29 + i)
 
     def gather2():
         for i, shift in enumerate((0, 32)):
             part = cur1.at[cur_rows(core, xo, 32, shift)]
-            landed(part, dp_recv.at[22 + i])
-            send(part, part, dp_send.at[27 + i], dp_recv.at[24], dev_core)
-            later(part, dp_send.at[27 + i])
+            landed(part, dp_recv.at[24 + i])
+            to_core(part, 31 + i)
 
     def gather3():
         other = pl.ds(pl.multiple_of((1 - core) * 256, 256), 256)
-        landed(cur1.at[other], dp_recv.at[24])
+        landed(cur1.at[other], dp_recv.at[26])
 
     def ls(j):
         lanes = pl.ds(pl.multiple_of((xo, xp, xm, x)[j] * 256, 256), 256)
@@ -450,15 +478,24 @@
             send(g.at[0, rows], q.at[i], fin_send.at[2 + i], fin_recv.at[5 + i], dev)
             later(q.at[i], fin_send.at[2 + i])
 
+    def last_hop(i, rows):
+        dev = (dev_xp, dev_xm)[i]
+        send(g.at[1 + i, rows], u.at[i, rows], fin_send.at[4 + i], fin_recv.at[7 + i], dev)
+
+    def lv():
+        for i in range(2):
+            part = both(1 + i)
+            rest = pl.ds(256 - 256 * i, 256)
+            fb[1 + i, core] = part
+            g[1 + i, rest] = part[256 - 256 * i : 512 - 256 * i].astype(BF16)
+            last_hop(i, rest)
+
     def lu():
-        for i, dev in enumerate((dev_xp, dev_xm)):
-            part = both(1 + i)
+        for i in range(2):
             landed(q.at[i], fin_recv.at[5 + i])
-            with_q, rest = pl.ds(256 * i, 256), pl.ds(256 - 256 * i, 256)
-            parts = part[:256], part[256:]
-            g[1 + i, rest] = parts[1 - i].astype(BF16)
-            g[1 + i, with_q] = (parts[i] + q[i].astype(F32)).astype(BF16)
-            send(g.at[1 + i], u.at[i], fin_send.at[4 + i], fin_recv.at[7 + i], dev)
+            rows = pl.ds(256 * i, 256)
+            g[1 + i, rows] = (fb[1 + i, core, rows, :] + q[i].astype(F32)).astype(BF16)
+            last_hop(i, rows)
             later(u.at[i], fin_send.at[4 + i])
 
     def cnt():
@@ -508,25 +545,29 @@
         rh=rh,
         update=update,
         gather1=gather1,
+        gather1b=gather1b,
         gather2=gather2,
         gather3=gather3,
         ls=ls,
         lq=lq,
         lu=lu,
+        lv=lv,
         cnt=cnt,
         own=own,
         fin=fin,
     )
     for name, *numbers in SCHEDULE:
         parts[name](*numbers)
-        if (name, *numbers) == ("zs", 0, 0):
+        if (name, *numbers) == ("zs", 0, 1):
             tables()
+            for load in loads:
+                load.wait()
         if (name, *numbers) == ("relay", 0, 0):
             tables_in()
 
 
 def on_device(points, candidates, centroids):
-    vmem = pl.BlockSpec(memory_space=pltpu.VMEM)
+    vmem, hbm = pl.BlockSpec(memory_space=pltpu.VMEM), pl.BlockSpec(memory_space=pl.ANY)
     sem = pltpu.SemaphoreType.DMA
     steps = points.shape[0]
     sums, counts = pl.pallas_call(
@@ -535,9 +576,11 @@
             jax.ShapeDtypeStruct((CBS, D // (NX * NC)), F32),
             jax.ShapeDtypeStruct((4, 128), F32),
         ),
-        in_specs=[vmem, pl.BlockSpec(memory_space=pltpu.SMEM), vmem],
+        in_specs=[hbm, pl.BlockSpec(memory_space=pltpu.SMEM), hbm],
         out_specs=(vmem, vmem),
         scratch_shapes=[
+            pltpu.VMEM((steps, NB, PB, D), BF16),
+            pltpu.VMEM((CBS, D), BF16),
             [pltpu.VMEM((NB, PB, D), BF16) for _ in range(7 * steps)],
             [pltpu.VMEM((64, PB, D), BF16) for _ in range(steps)],
             [pltpu.VMEM((NZ, 6, PB, D), BF16) for _ in range(steps)],
@@ -575,15 +618,16 @@
             sem((steps, NZ)),
             sem((steps, 6)),
             sem((3,)),
-            sem((29,)),
-            sem((25,)),
+            sem((33,)),
+            sem((27,)),
             sem((6,)),
             sem((9,)),
+            sem((2,)),
         ],
         compiler_params=pltpu.CompilerParams(
             collective_id=0, has_side_effects=True, vmem_limit_bytes=56 * 1024 * 1024
         ),
-    )(points.reshape(steps, NB, PB, D), candidates, centroids)
+    )(points.reshape(steps, NB, PB, D), jnp.transpose(candidates, (0, 2, 1)), centroids)
     return sums, counts.reshape(CBS)
 
 

time: 156 us -> 150 us (0.962)
  Pallas kernels: 152 us -> 147 us
    pallas_call x1, Pallas kernels: 152 us -> 147 us  [on_device(): pl.pallas_call(kernel, out_shape=(jax.ShapeDtypeStruct((CBS, D // (NX * N...]
    unnamed x5 -> x4, local copies, waits for them, and re-layouts: 3.62 us -> 2.25 us
where the time goes in v2:
time: 150 us
  Pallas kernels  147 us (98%)
  local copies, waits for them, and re-layouts  2.25 us (2%)
    pallas_call x1, Pallas kernels, on_device(): pl.pallas_call(kernel, out_shape=(jax.ShapeDtypeStruct((CBS, D // (NX * N...  147 us

profile of v2, /device:TPU:2, one launch (start us, length us, event | category | flops | bytes accessed | tf_op | source)
XLA Modules:
  0.0 149.7 jit_solution(17497259043935693237)
XLA Ops:
  0.6 146.8 %shard_map.50 = (f32[512,128]{1,0:T(8,128)}, f32[4,128]{1,0:T(4,128)}) custom-call(bf16[2,8,32,1024]{3,2,1,0:T(8,128)(2,1)} %bitcast.3, s32[2,4,8]{2,1,0:T(4,128)} %bitcast.4, bf16[512,1024]{1,0:T(8,128)(2,1)} %cent_hbm.1), custom_call_target="tpu_custom_call" | custom-call | tf_op jit(solution)/shard_map/pallas_call | solution.py:573
  147.4 0.0 copy-start
  147.4 1.7 %copy.7 = f32[512,128]{1,0:T(8,128)} copy(f32[512,128]{1,0:T(8,128)} %get-tuple-element.8) | data formatting | bytes 524288
  149.1 0.0 copy-done
  149.1 0.6 copy.8
Async XLA Ops:
  147.4 1.7 %copy-start = (f32[4,128]{1,0:T(4,128)S(1)}, f32[4,128]{1,0:T(4,128)}, u32[]{:S(2)}) copy-start(f32[4,128]{1,0:T(4,128)} %get-tuple-element.5) | copy-start | bytes 6148

commit v3 on v2

--- a/solution.py
+++ b/solution.py
@@ -14,21 +14,21 @@
 PLUS = ((1, 0), (1, 1), (2, 0), (2, 1), (3, 0), (3, 1), (4, 0))
 MINUS = ((7, 1), (7, 0), (6, 1), (6, 0), (5, 1), (5, 0), (4, 1))
 SCHEDULE = (
-    ("zs", 0, 0), ("zs", 0, 1), ("pick", 0, 0), ("pick", 1, 0), ("relay", 0, 0), ("ze", 0, 0, 0), ("ze", 0, 1, 0),
+    ("zs", 0, 0), ("pick", 0, 0), ("pick", 1, 0), ("zs", 0, 1), ("relay", 0, 0), ("ze", 0, 0, 0), ("ze", 0, 1, 0),
     ("relay", 1, 0), ("score", 0, 0), ("ze", 0, 0, 1), ("ze", 0, 1, 1), ("pick", 0, 1), ("pick", 0, 7),
-    ("relay", 0, 1), ("ze", 0, 0, 2), ("ze", 0, 1, 2), ("relay", 0, 7), ("ze", 0, 0, 3), ("pick", 0, 2),
-    ("ze", 0, 1, 3), ("pick", 0, 6), ("score", 0, 1), ("score", 0, 7), ("relay", 0, 2), ("ze", 0, 0, 4),
-    ("ze", 0, 1, 4), ("relay", 0, 6), ("ze", 0, 0, 5), ("pick", 0, 3), ("ze", 0, 1, 5), ("pick", 0, 5),
-    ("score", 0, 2), ("score", 0, 6), ("relay", 0, 3), ("ze", 0, 0, 6), ("ze", 0, 1, 6), ("zs", 1, 0), ("zs", 1, 1),
-    ("pick", 0, 4), ("relay", 0, 5), ("ze", 1, 0, 0), ("ze", 1, 1, 0), ("score", 0, 3), ("relay", 0, 4),
-    ("ze", 1, 0, 1), ("pick", 1, 1), ("ze", 1, 1, 1), ("pick", 1, 7), ("score", 0, 5), ("score", 0, 4), ("share", 0),
-    ("relay", 1, 1), ("partial", 0), ("ze", 1, 0, 2), ("ze", 1, 1, 2), ("relay", 1, 7), ("whole", 0), ("ze", 1, 0, 3),
-    ("pick", 1, 2), ("ze", 1, 1, 3), ("pick", 1, 6), ("weigh", 0), ("rf", 0), ("ro", 0), ("rf", 1), ("ro", 1),
-    ("relay", 1, 2), ("rc", 0), ("rf", 2), ("rc", 1), ("ze", 1, 0, 4), ("ze", 1, 1, 4), ("ro", 2), ("rh", 0),
-    ("rf", 3), ("rc", 2), ("rh", 1), ("relay", 1, 6), ("ro", 3), ("rc", 3), ("rh", 2), ("ze", 1, 0, 5), ("pick", 1, 3),
-    ("ze", 1, 1, 5), ("pick", 1, 5), ("rh", 3), ("update",), ("relay", 1, 3), ("ze", 1, 0, 6), ("ze", 1, 1, 6),
-    ("pick", 1, 4), ("gather1",), ("gather1b",), ("relay", 1, 5), ("gather2",), ("gather3",), ("score", 1, 0),
-    ("score", 1, 1), ("score", 1, 7), ("score", 1, 2), ("relay", 1, 4), ("score", 1, 6), ("score", 1, 3),
+    ("relay", 0, 1), ("ze", 0, 0, 2), ("ze", 0, 1, 2), ("relay", 0, 7), ("ze", 0, 0, 3), ("ze", 0, 1, 3),
+    ("pick", 0, 2), ("pick", 0, 6), ("score", 0, 1), ("score", 0, 7), ("relay", 0, 2), ("ze", 0, 0, 4),
+    ("ze", 0, 1, 4), ("relay", 0, 6), ("ze", 0, 0, 5), ("pick", 0, 3), ("ze", 0, 1, 5), ("zs", 1, 0), ("pick", 0, 5),
+    ("score", 0, 2), ("score", 0, 6), ("relay", 0, 3), ("ze", 0, 0, 6), ("ze", 0, 1, 6), ("zs", 1, 1), ("pick", 0, 4),
+    ("relay", 0, 5), ("ze", 1, 0, 0), ("ze", 1, 1, 0), ("score", 0, 3), ("relay", 0, 4), ("ze", 1, 0, 1),
+    ("ze", 1, 1, 1), ("pick", 1, 1), ("pick", 1, 7), ("score", 0, 5), ("score", 0, 4), ("share", 0), ("relay", 1, 1),
+    ("partial", 0), ("ze", 1, 0, 2), ("ze", 1, 1, 2), ("relay", 1, 7), ("whole", 0), ("ze", 1, 0, 3), ("ze", 1, 1, 3),
+    ("pick", 1, 2), ("pick", 1, 6), ("weigh", 0), ("rf", 0), ("ro", 0), ("relay", 1, 2), ("rf", 1), ("ro", 1),
+    ("rc", 0), ("rf", 2), ("ro", 2), ("rc", 1), ("ze", 1, 0, 4), ("ze", 1, 1, 4), ("rh", 0), ("rf", 3),
+    ("relay", 1, 6), ("rc", 2), ("rh", 1), ("ro", 3), ("rc", 3), ("rh", 2), ("ze", 1, 0, 5), ("pick", 1, 3),
+    ("ze", 1, 1, 5), ("pick", 1, 5), ("rh", 3), ("relay", 1, 3), ("update",), ("ze", 1, 0, 6), ("ze", 1, 1, 6),
+    ("pick", 1, 4), ("gather1",), ("relay", 1, 5), ("gather1b",), ("gather2",), ("gather3",), ("score", 1, 0),
+    ("score", 1, 1), ("score", 1, 7), ("relay", 1, 4), ("score", 1, 2), ("score", 1, 6), ("score", 1, 3),
     ("score", 1, 5), ("score", 1, 4), ("share", 1), ("partial", 1), ("whole", 1), ("weigh", 1), ("ls", 0), ("ls", 1),
     ("ls", 2), ("lq",), ("ls", 3), ("cnt",), ("lv",), ("lu",), ("own",), ("fin",),
 )
@@ -131,12 +131,6 @@
         copy.start()
         return copy
 
-    def send_cut(src, dst, ssem, rsem, dev):
-        size = src.shape[0] // 2
-        for i in range(2):
-            part = pl.ds(i * size, size)
-            send(src.at[part], dst.at[part], ssem, rsem, dev)
-
     def landed(ref, sem):
         pltpu.make_async_copy(ref, ref, sem).wait()
 
@@ -154,13 +148,12 @@
     def chunk(step, k):
         return pts.at[step] if k == 0 else zbufs[step * 7 + k - 1]
 
-    def z_start(step, d):
-        order = (PLUS, MINUS)[d]
-        for i in range(2):
+    def z_start(step, i):
+        for d, order in enumerate((PLUS, MINUS)):
             k, h = order[i]
             src = half(pts_hbm.at[step], h)
             dst = half(chunk(step, k), h)
-            send_cut(src, dst, z_send.at[step, d, i], z_recv.at[step, d, i], z_devs[d])
+            send(src, dst, z_send.at[step, d, i], z_recv.at[step, d, i], z_devs[d])
             later(src, z_send.at[step, d, i])
 
     def z_event(step, d, i):
@@ -170,7 +163,7 @@
         landed(here, z_recv.at[step, d, i])
         if i < 5:
             dst = half(chunk(step, order[i + 2][0]), h)
-            send_cut(here, dst, z_send.at[step, d, i + 2], z_recv.at[step, d, i + 2], z_devs[d])
+            send(here, dst, z_send.at[step, d, i + 2], z_recv.at[step, d, i + 2], z_devs[d])
             later(here, z_send.at[step, d, i + 2])
 
     def tables():
@@ -225,7 +218,7 @@
             first = 0 if p == 1 else 4
             box[k, first] = block(p, 0)
             box[k, first + 1] = block(p, 1)
-            send_cut(
+            send(
                 box.at[k, pl.ds(first, 2)], xr.at[pl.ds(k * 8 + p * 2, 2)], sems[0], sems[1], dev
             )
         later(box.at[k], sems[0])
@@ -558,7 +551,7 @@
     )
     for name, *numbers in SCHEDULE:
         parts[name](*numbers)
-        if (name, *numbers) == ("zs", 0, 1):
+        if (name, *numbers) == ("zs", 0, 0):
             tables()
             for load in loads:
                 load.wait()

time: 150 us -> 146 us (0.973)
  Pallas kernels: 147 us -> 143 us
    pallas_call x1, Pallas kernels: 147 us -> 143 us  [on_device(): pl.pallas_call(kernel, out_shape=(jax.ShapeDtypeStruct((CBS, D // (NX * N...]
where the time goes in v3:
time: 146 us
  Pallas kernels  143 us (98%)
  local copies, waits for them, and re-layouts  2.25 us (2%)
    pallas_call x1, Pallas kernels, on_device(): pl.pallas_call(kernel, out_shape=(jax.ShapeDtypeStruct((CBS, D // (NX * N...  143 us

profile of v3, /device:TPU:2, one launch (start us, length us, event | category | flops | bytes accessed | tf_op | source)
XLA Modules:
  0.0 146.1 jit_solution(10813915119561523799)
XLA Ops:
  0.6 143.2 %shard_map.50 = (f32[512,128]{1,0:T(8,128)}, f32[4,128]{1,0:T(4,128)}) custom-call(bf16[2,8,32,1024]{3,2,1,0:T(8,128)(2,1)} %bitcast.3, s32[2,4,8]{2,1,0:T(4,128)} %bitcast.4, bf16[512,1024]{1,0:T(8,128)(2,1)} %cent_hbm.1), custom_call_target="tpu_custom_call" | custom-call | tf_op jit(solution)/shard_map/pallas_call | solution.py:566
  143.9 0.0 copy-start
  143.9 1.7 %copy.7 = f32[512,128]{1,0:T(8,128)} copy(f32[512,128]{1,0:T(8,128)} %get-tuple-element.8) | data formatting | bytes 524288
  145.5 0.0 copy-done
  145.5 0.6 copy.8
Async XLA Ops:
  143.9 1.7 %copy-start = (f32[4,128]{1,0:T(4,128)S(1)}, f32[4,128]{1,0:T(4,128)}, u32[]{:S(2)}) copy-start(f32[4,128]{1,0:T(4,128)} %get-tuple-element.5) | copy-start | bytes 6148

commit v4 on v3

--- a/solution.py
+++ b/solution.py
@@ -14,23 +14,24 @@
 PLUS = ((1, 0), (1, 1), (2, 0), (2, 1), (3, 0), (3, 1), (4, 0))
 MINUS = ((7, 1), (7, 0), (6, 1), (6, 0), (5, 1), (5, 0), (4, 1))
 SCHEDULE = (
-    ("zs", 0, 0), ("pick", 0, 0), ("pick", 1, 0), ("zs", 0, 1), ("relay", 0, 0), ("ze", 0, 0, 0), ("ze", 0, 1, 0),
-    ("relay", 1, 0), ("score", 0, 0), ("ze", 0, 0, 1), ("ze", 0, 1, 1), ("pick", 0, 1), ("pick", 0, 7),
-    ("relay", 0, 1), ("ze", 0, 0, 2), ("ze", 0, 1, 2), ("relay", 0, 7), ("ze", 0, 0, 3), ("ze", 0, 1, 3),
-    ("pick", 0, 2), ("pick", 0, 6), ("score", 0, 1), ("score", 0, 7), ("relay", 0, 2), ("ze", 0, 0, 4),
-    ("ze", 0, 1, 4), ("relay", 0, 6), ("ze", 0, 0, 5), ("pick", 0, 3), ("ze", 0, 1, 5), ("zs", 1, 0), ("pick", 0, 5),
-    ("score", 0, 2), ("score", 0, 6), ("relay", 0, 3), ("ze", 0, 0, 6), ("ze", 0, 1, 6), ("zs", 1, 1), ("pick", 0, 4),
-    ("relay", 0, 5), ("ze", 1, 0, 0), ("ze", 1, 1, 0), ("score", 0, 3), ("relay", 0, 4), ("ze", 1, 0, 1),
-    ("ze", 1, 1, 1), ("pick", 1, 1), ("pick", 1, 7), ("score", 0, 5), ("score", 0, 4), ("share", 0), ("relay", 1, 1),
-    ("partial", 0), ("ze", 1, 0, 2), ("ze", 1, 1, 2), ("relay", 1, 7), ("whole", 0), ("ze", 1, 0, 3), ("ze", 1, 1, 3),
-    ("pick", 1, 2), ("pick", 1, 6), ("weigh", 0), ("rf", 0), ("ro", 0), ("relay", 1, 2), ("rf", 1), ("ro", 1),
-    ("rc", 0), ("rf", 2), ("ro", 2), ("rc", 1), ("ze", 1, 0, 4), ("ze", 1, 1, 4), ("rh", 0), ("rf", 3),
-    ("relay", 1, 6), ("rc", 2), ("rh", 1), ("ro", 3), ("rc", 3), ("rh", 2), ("ze", 1, 0, 5), ("pick", 1, 3),
-    ("ze", 1, 1, 5), ("pick", 1, 5), ("rh", 3), ("relay", 1, 3), ("update",), ("ze", 1, 0, 6), ("ze", 1, 1, 6),
-    ("pick", 1, 4), ("gather1",), ("relay", 1, 5), ("gather1b",), ("gather2",), ("gather3",), ("score", 1, 0),
-    ("score", 1, 1), ("score", 1, 7), ("relay", 1, 4), ("score", 1, 2), ("score", 1, 6), ("score", 1, 3),
-    ("score", 1, 5), ("score", 1, 4), ("share", 1), ("partial", 1), ("whole", 1), ("weigh", 1), ("ls", 0), ("ls", 1),
-    ("ls", 2), ("lq",), ("ls", 3), ("cnt",), ("lv",), ("lu",), ("own",), ("fin",),
+    ("zs", 0, 0), ("pick", 0, 0), ("pick", 1, 0), ("zs", 0, 1), ("relay", 0, 0), ("relay", 1, 0), ("ze", 0, 0, 0),
+    ("ze", 0, 1, 0), ("score", 0), ("ze", 0, 1, 1), ("ze", 0, 0, 1), ("pick", 0, 7), ("pick", 0, 1), ("ze", 0, 0, 2),
+    ("relay", 0, 7), ("ze", 0, 1, 2), ("relay", 0, 1), ("ze", 0, 0, 3), ("pick", 0, 2), ("score", 1), ("ze", 0, 1, 3),
+    ("pick", 0, 6), ("score", 7), ("ze", 0, 0, 4), ("relay", 0, 2), ("ze", 0, 1, 4), ("relay", 0, 6), ("ze", 0, 0, 5),
+    ("pick", 0, 3), ("ze", 0, 1, 5), ("score", 2), ("pick", 0, 5), ("zs", 1, 0), ("relay", 0, 3), ("ze", 0, 0, 6),
+    ("ze", 0, 1, 6), ("pick", 0, 4), ("zs", 1, 1), ("relay", 0, 5), ("score", 3), ("ze", 1, 0, 0), ("ze", 1, 1, 0),
+    ("relay", 0, 4), ("score", 6), ("score", 5), ("ze", 1, 1, 1), ("pick", 1, 7), ("ze", 1, 0, 1), ("score", 4),
+    ("share", 0), ("pick", 1, 1), ("partial", 0), ("ze", 1, 1, 2), ("relay", 1, 7), ("relay", 1, 1), ("ze", 1, 0, 2),
+    ("whole", 0), ("ze", 1, 0, 3), ("ze", 1, 1, 3), ("pick", 1, 2), ("pick", 1, 6), ("weigh", 0), ("rf", 0), ("ro", 0),
+    ("rf", 1), ("ro", 1), ("rf", 2), ("ro", 2), ("rc", 0), ("rf", 3), ("relay", 1, 6), ("rc", 1), ("ro", 3), ("rc", 2),
+    ("relay", 1, 2), ("ze", 1, 0, 4), ("ze", 1, 0, 5), ("ze", 1, 1, 4), ("ze", 1, 1, 5), ("rc", 3), ("pick", 1, 5),
+    ("rh", 0), ("rh", 2), ("rh", 1), ("pick", 1, 3), ("rh", 3), ("update",), ("ze", 1, 0, 6), ("relay", 1, 3),
+    ("gw", 0), ("sc", 0, 7), ("sc", 0, 0), ("ze", 1, 1, 6), ("pick", 1, 4), ("sc", 0, 2), ("gather1",), ("gather1b",),
+    ("sc", 0, 6), ("sc", 0, 1), ("relay", 1, 5), ("gw", 1), ("sc", 1, 0), ("sc", 1, 1), ("gather2",), ("sc", 1, 6),
+    ("sc", 1, 7), ("sc", 1, 2), ("sc", 0, 3), ("relay", 1, 4), ("sc", 1, 3), ("gw", 2), ("sc", 2, 3), ("sc", 2, 2),
+    ("sc", 2, 7), ("sc", 2, 1), ("sc", 0, 5), ("sc", 2, 0), ("sc", 2, 6), ("sc", 1, 5), ("sc", 2, 5), ("sc", 0, 4),
+    ("sc", 1, 4), ("sc", 2, 4), ("share", 1), ("partial", 1), ("whole", 1), ("weigh", 1), ("ls", 0), ("ls", 1),
+    ("ls", 2), ("ls", 3), ("lq",), ("cnt",), ("lv",), ("lu",), ("own",), ("fin",),
 )
 
 
@@ -51,6 +52,8 @@
     tab_sm,
     scores,
     tops,
+    tops4,
+    totals4,
     w,
     lses,
     stats,
@@ -238,21 +241,51 @@
             )
         later(relays[step].at[k], r_send.at[step, k])
 
-    def score(step, k):
-        xr, centroids = xs[step], (cent, cur1)[step]
-        landed(xr.at[pl.ds(k * 8 + 2, 6)], x_recv.at[step, k])
-        rows = xr[k * 8 : k * 8 + 8].reshape(8 * PB, D)
-        s = lax.dot_general(
-            centroids[...], rows, (((1,), (1,)), ((), ())), preferred_element_type=F32
+    def arrived(step, k):
+        landed(xs[step].at[pl.ds(k * 8 + 2, 6)], x_recv.at[step, k])
+
+    def against(step, k, centroids):
+        rows = xs[step][k * 8 : k * 8 + 8].reshape(8 * PB, D)
+        return lax.dot_general(
+            centroids, rows, (((1,), (1,)), ((), ())), preferred_element_type=F32
         )
+
+    def exps(s):
         top = jnp.max(s, axis=0, keepdims=True)
         e = jnp.exp(s - top)
+        return e, top, jnp.sum(e, axis=0, keepdims=True)
+
+    def keep(step, k, lse):
+        for i in range(2):
+            lses[step][i, k : k + 1, :] = lse[:, i * 128 : (i + 1) * 128]
+
+    def score(k):
+        arrived(0, k)
+        e, top, total = exps(against(0, k, cent[...]))
         scores[k] = e
         tops[k] = top
-        total = jnp.sum(e, axis=0, keepdims=True)
-        lse = top + jnp.log(total)
-        for i in range(2):
-            lses[step][i, k : k + 1, :] = lse[:, i * 128 : (i + 1) * 128]
+        keep(0, k, top + jnp.log(total))
+
+    def sc(part, k):
+        if part == 0:
+            arrived(1, k)
+        which = ((x,), (xm, xp), (xo,))[part]
+        places = [cur_rows(c, at) for at in which for c in range(2)]
+        s = against(1, k, jnp.concatenate([cur1[rows, :] for rows in places], axis=0))
+        for i, at in enumerate(which):
+            e, top, total = exps(s[i * 128 : i * 128 + 128])
+            scores[k, places[2 * i], :] = e[:64]
+            scores[k, places[2 * i + 1], :] = e[64:]
+            tops4[at, k] = top
+            totals4[at, k] = total
+
+    def join():
+        for k in range(NZ):
+            top = jnp.maximum(
+                jnp.maximum(tops4[0, k], tops4[1, k]), jnp.maximum(tops4[2, k], tops4[3, k])
+            )
+            total = sum(totals4[i, k] * jnp.exp(tops4[i, k] - top) for i in range(NX))
+            keep(1, k, top + jnp.log(total))
 
     low = lax.broadcasted_iota(jnp.int32, (1, 128), 1) < 64
     group = lax.broadcasted_iota(jnp.int32, (1, 128), 1) >> 5
@@ -268,6 +301,8 @@
         ]
 
     def share(step):
+        if step == 1:
+            join()
         for p in range(1, NY):
             send(
                 lses[step].at[p >> 1],
@@ -348,8 +383,16 @@
             for t in range(2):
                 shift = jnp.where(low, back[2 * t, k : k + 1, :], back[2 * t + 1, k : k + 1, :])
                 lanes = pl.ds(k * 256 + t * 128, 128)
-                scale = jnp.exp(tops[k, :, t * 128 : (t + 1) * 128] - shift)
-                w[:, lanes] = (scores[k, :, t * 128 : (t + 1) * 128] * scale).astype(BF16)
+                half_lanes = slice(t * 128, (t + 1) * 128)
+                if step == 0:
+                    scale = jnp.exp(tops[k, :, half_lanes] - shift)
+                    w[:, lanes] = (scores[k, :, half_lanes] * scale).astype(BF16)
+                    continue
+                for at in range(NX):
+                    scale = jnp.exp(tops4[at, k, :, half_lanes] - shift)
+                    for first in (at * 64, 256 + at * 64):
+                        rows = slice(first, first + 64)
+                        w[rows, lanes] = (scores[k, rows, half_lanes] * scale).astype(BF16)
 
     def half_sums(which, n):
         rows = w[pl.ds(pl.multiple_of(which * 256, 256), 256), :]
@@ -419,10 +462,10 @@
             send(part, part, dp_send.at[sem], dp_recv.at[sem], dev)
             later(part, dp_send.at[sem])
             if i == 1:
-                to_core(cur1.at[mine], 24)
-
-    def to_core(part, sem):
-        send(part, part, dp_send.at[sem], dp_recv.at[26], dev_core)
+                to_core(cur1.at[mine], 24, 0)
+
+    def to_core(part, sem, group):
+        send(part, part, dp_send.at[sem], dp_recv.at[26 + group], dev_core)
         later(part, dp_send.at[sem])
 
     def gather1():
@@ -431,23 +474,22 @@
             landed(part, dp_recv.at[20 + i])
             send(part, part, dp_send.at[25 + i], dp_recv.at[24 + i], dev)
             later(part, dp_send.at[25 + i])
-            to_core(part, 27 + i)
+            to_core(part, 27 + i, 1)
 
     def gather1b():
         for i, (at, shift) in enumerate(((xm, 32), (xp, 0))):
             part = cur1.at[cur_rows(core, at, 32, shift)]
             landed(part, dp_recv.at[22 + i])
-            to_core(part, 29 + i)
+            to_core(part, 29 + i, 1)
 
     def gather2():
         for i, shift in enumerate((0, 32)):
             part = cur1.at[cur_rows(core, xo, 32, shift)]
             landed(part, dp_recv.at[24 + i])
-            to_core(part, 31 + i)
-
-    def gather3():
-        other = pl.ds(pl.multiple_of((1 - core) * 256, 256), 256)
-        landed(cur1.at[other], dp_recv.at[26])
+            to_core(part, 31 + i, 2)
+
+    def gw(group):
+        landed(cur1.at[pl.ds(0, (64, 128, 64)[group])], dp_recv.at[26 + group])
 
     def ls(j):
         lanes = pl.ds(pl.multiple_of((xo, xp, xm, x)[j] * 256, 256), 256)
@@ -540,7 +582,8 @@
         gather1=gather1,
         gather1b=gather1b,
         gather2=gather2,
-        gather3=gather3,
+        gw=gw,
+        sc=sc,
         ls=ls,
         lq=lq,
         lu=lu,
@@ -583,6 +626,8 @@
             pltpu.SMEM((NZ, 1, 512), jnp.int32),
             pltpu.VMEM((NZ, CBS, 256), F32),
             pltpu.VMEM((NZ, 1, 256), F32),
+            pltpu.VMEM((NX, NZ, 1, 256), F32),
+            pltpu.VMEM((NX, NZ, 1, 256), F32),
             pltpu.VMEM((CBS, 64 * PB), BF16),
             [pltpu.VMEM((2, 8, 128), F32) for _ in range(steps)],
             [pltpu.VMEM((4, 8, 128), F32) for _ in range(steps)],
@@ -612,7 +657,7 @@
             sem((steps, 6)),
             sem((3,)),
             sem((33,)),
-            sem((27,)),
+            sem((29,)),
             sem((6,)),
             sem((9,)),
             sem((2,)),

time: 146 us -> 141 us (0.966)
  Pallas kernels: 143 us -> 138 us
    pallas_call x1, Pallas kernels: 143 us -> 138 us  [on_device(): pl.pallas_call(kernel, out_shape=(jax.ShapeDtypeStruct((CBS, D // (NX * N...]
where the time goes in v4:
time: 141 us; the launch traced here: 140 us
  Pallas kernels  138 us (98%)
  local copies, waits for them, and re-layouts  2.25 us (2%)
    pallas_call x1, Pallas kernels, on_device(): pl.pallas_call(kernel, out_shape=(jax.ShapeDtypeStruct((CBS, D // (NX * N...  138 us

profile of v4, /device:TPU:2, one launch (start us, length us, event | category | flops | bytes accessed | tf_op | source)
XLA Modules:
  0.0 140.4 jit_solution(6107306857722680892)
XLA Ops:
  0.6 137.5 %shard_map.50 = (f32[512,128]{1,0:T(8,128)}, f32[4,128]{1,0:T(4,128)}) custom-call(bf16[2,8,32,1024]{3,2,1,0:T(8,128)(2,1)} %bitcast.3, s32[2,4,8]{2,1,0:T(4,128)} %bitcast.4, bf16[512,1024]{1,0:T(8,128)(2,1)} %cent_hbm.1), custom_call_target="tpu_custom_call" | custom-call | tf_op jit(solution)/shard_map/pallas_call | solution.py:609
  138.2 0.0 copy-start
  138.2 1.7 %copy.7 = f32[512,128]{1,0:T(8,128)} copy(f32[512,128]{1,0:T(8,128)} %get-tuple-element.8) | data formatting | bytes 524288
  139.8 0.0 copy-done
  139.9 0.6 copy.8
Async XLA Ops:
  138.2 1.7 %copy-start = (f32[4,128]{1,0:T(4,128)S(1)}, f32[4,128]{1,0:T(4,128)}, u32[]{:S(2)}) copy-start(f32[4,128]{1,0:T(4,128)} %get-tuple-element.5) | copy-start | bytes 6148

commit v5 on v4

--- a/solution.py
+++ b/solution.py
@@ -14,24 +14,27 @@
 PLUS = ((1, 0), (1, 1), (2, 0), (2, 1), (3, 0), (3, 1), (4, 0))
 MINUS = ((7, 1), (7, 0), (6, 1), (6, 0), (5, 1), (5, 0), (4, 1))
 SCHEDULE = (
-    ("zs", 0, 0), ("pick", 0, 0), ("pick", 1, 0), ("zs", 0, 1), ("relay", 0, 0), ("relay", 1, 0), ("ze", 0, 0, 0),
-    ("ze", 0, 1, 0), ("score", 0), ("ze", 0, 1, 1), ("ze", 0, 0, 1), ("pick", 0, 7), ("pick", 0, 1), ("ze", 0, 0, 2),
-    ("relay", 0, 7), ("ze", 0, 1, 2), ("relay", 0, 1), ("ze", 0, 0, 3), ("pick", 0, 2), ("score", 1), ("ze", 0, 1, 3),
-    ("pick", 0, 6), ("score", 7), ("ze", 0, 0, 4), ("relay", 0, 2), ("ze", 0, 1, 4), ("relay", 0, 6), ("ze", 0, 0, 5),
-    ("pick", 0, 3), ("ze", 0, 1, 5), ("score", 2), ("pick", 0, 5), ("zs", 1, 0), ("relay", 0, 3), ("ze", 0, 0, 6),
-    ("ze", 0, 1, 6), ("pick", 0, 4), ("zs", 1, 1), ("relay", 0, 5), ("score", 3), ("ze", 1, 0, 0), ("ze", 1, 1, 0),
-    ("relay", 0, 4), ("score", 6), ("score", 5), ("ze", 1, 1, 1), ("pick", 1, 7), ("ze", 1, 0, 1), ("score", 4),
-    ("share", 0), ("pick", 1, 1), ("partial", 0), ("ze", 1, 1, 2), ("relay", 1, 7), ("relay", 1, 1), ("ze", 1, 0, 2),
-    ("whole", 0), ("ze", 1, 0, 3), ("ze", 1, 1, 3), ("pick", 1, 2), ("pick", 1, 6), ("weigh", 0), ("rf", 0), ("ro", 0),
-    ("rf", 1), ("ro", 1), ("rf", 2), ("ro", 2), ("rc", 0), ("rf", 3), ("relay", 1, 6), ("rc", 1), ("ro", 3), ("rc", 2),
-    ("relay", 1, 2), ("ze", 1, 0, 4), ("ze", 1, 0, 5), ("ze", 1, 1, 4), ("ze", 1, 1, 5), ("rc", 3), ("pick", 1, 5),
-    ("rh", 0), ("rh", 2), ("rh", 1), ("pick", 1, 3), ("rh", 3), ("update",), ("ze", 1, 0, 6), ("relay", 1, 3),
-    ("gw", 0), ("sc", 0, 7), ("sc", 0, 0), ("ze", 1, 1, 6), ("pick", 1, 4), ("sc", 0, 2), ("gather1",), ("gather1b",),
-    ("sc", 0, 6), ("sc", 0, 1), ("relay", 1, 5), ("gw", 1), ("sc", 1, 0), ("sc", 1, 1), ("gather2",), ("sc", 1, 6),
-    ("sc", 1, 7), ("sc", 1, 2), ("sc", 0, 3), ("relay", 1, 4), ("sc", 1, 3), ("gw", 2), ("sc", 2, 3), ("sc", 2, 2),
-    ("sc", 2, 7), ("sc", 2, 1), ("sc", 0, 5), ("sc", 2, 0), ("sc", 2, 6), ("sc", 1, 5), ("sc", 2, 5), ("sc", 0, 4),
-    ("sc", 1, 4), ("sc", 2, 4), ("share", 1), ("partial", 1), ("whole", 1), ("weigh", 1), ("ls", 0), ("ls", 1),
-    ("ls", 2), ("ls", 3), ("lq",), ("cnt",), ("lv",), ("lu",), ("own",), ("fin",),
+    ("zs", 0, 0, 0), ("pr", 0, 0), ("zs", 0, 0, 1), ("pp", 0, 0), ("pr", 1, 0), ("pp", 1, 0), ("zs", 0, 1, 0),
+    ("relay", 0, 0), ("zs", 0, 1, 1), ("relay", 1, 0), ("ze", 0, 0, 0), ("ze", 0, 1, 0), ("ze", 0, 0, 1), ("pr", 0, 1),
+    ("pp", 0, 1), ("ze", 0, 1, 1), ("pr", 0, 7), ("pp", 0, 7), ("ze", 0, 0, 2), ("relay", 0, 1), ("relay", 0, 7),
+    ("ze", 0, 1, 2), ("ze", 0, 0, 3), ("pr", 0, 2), ("pp", 0, 2), ("score", 1), ("score", 0), ("ze", 0, 1, 3),
+    ("pr", 0, 6), ("relay", 0, 2), ("pp", 0, 6), ("ze", 0, 0, 4), ("relay", 0, 6), ("score", 7), ("ze", 0, 1, 4),
+    ("ze", 0, 0, 5), ("pr", 0, 3), ("pp", 0, 3), ("ze", 0, 1, 5), ("score", 2), ("zs", 1, 0, 0), ("pr", 0, 5),
+    ("zs", 1, 1, 0), ("relay", 0, 3), ("pp", 0, 5), ("score", 6), ("zs", 1, 1, 1), ("ze", 0, 1, 6), ("ze", 0, 0, 6),
+    ("pr", 0, 4), ("zs", 1, 0, 1), ("relay", 0, 5), ("pp", 0, 4), ("score", 3), ("relay", 0, 4), ("ze", 1, 0, 0),
+    ("ze", 1, 1, 0), ("score", 5), ("ze", 1, 1, 1), ("pr", 1, 7), ("pp", 1, 7), ("score", 4), ("share", 0),
+    ("ze", 1, 0, 1), ("pr", 1, 1), ("pp", 1, 1), ("partial", 0), ("relay", 1, 7), ("ze", 1, 1, 2), ("ze", 1, 0, 2),
+    ("relay", 1, 1), ("whole", 0), ("ze", 1, 1, 3), ("pr", 1, 6), ("pp", 1, 6), ("ze", 1, 0, 3), ("pr", 1, 2),
+    ("pp", 1, 2), ("weigh", 0), ("rf", 0), ("ro", 0), ("rf", 1), ("ro", 1), ("rf", 2), ("ro", 2), ("rc", 0), ("re", 0),
+    ("rf", 3), ("rc", 1), ("re", 1), ("relay", 1, 6), ("rc", 2), ("relay", 1, 2), ("re", 2), ("ro", 3), ("rc", 3),
+    ("re", 3), ("ze", 1, 1, 4), ("ze", 1, 0, 4), ("ze", 1, 1, 5), ("pr", 1, 5), ("rh", 1), ("pp", 1, 5), ("rh", 0),
+    ("rh", 2), ("ze", 1, 0, 5), ("rh", 3), ("pr", 1, 3), ("pp", 1, 3), ("update",), ("ze", 1, 0, 6), ("ze", 1, 1, 6),
+    ("ub",), ("gw", 0), ("sc", 0, 6), ("relay", 1, 3), ("sc", 0, 7), ("sc", 0, 2), ("sc", 0, 0), ("gather1",),
+    ("gather1b",), ("pr", 1, 4), ("sc", 0, 1), ("relay", 1, 5), ("pp", 1, 4), ("sc", 0, 3), ("gw", 1), ("sc", 1, 6),
+    ("sc", 1, 0), ("gather2",), ("sc", 1, 2), ("sc", 1, 1), ("sc", 1, 3), ("relay", 1, 4), ("sc", 1, 7), ("gw", 2),
+    ("sc", 2, 2), ("sc", 2, 1), ("sc", 0, 5), ("sc", 1, 5), ("sc", 2, 3), ("sc", 2, 0), ("sc", 2, 7), ("sc", 2, 5),
+    ("sc", 0, 4), ("sc", 2, 4), ("sc", 1, 4), ("sc", 2, 6), ("share", 1), ("partial", 1), ("whole", 1), ("weigh", 1),
+    ("ls", 0), ("ls", 1), ("ls", 2), ("lq",), ("ls", 3), ("lv",), ("cnt",), ("lu",), ("own",), ("fin",),
 )
 
 
@@ -151,13 +154,12 @@
     def chunk(step, k):
         return pts.at[step] if k == 0 else zbufs[step * 7 + k - 1]
 
-    def z_start(step, i):
-        for d, order in enumerate((PLUS, MINUS)):
-            k, h = order[i]
-            src = half(pts_hbm.at[step], h)
-            dst = half(chunk(step, k), h)
-            send(src, dst, z_send.at[step, d, i], z_recv.at[step, d, i], z_devs[d])
-            later(src, z_send.at[step, d, i])
+    def z_start(step, d, i):
+        k, h = (PLUS, MINUS)[d][i]
+        src = half(pts_hbm.at[step], h)
+        dst = half(chunk(step, k), h)
+        send(src, dst, z_send.at[step, d, i], z_recv.at[step, d, i], z_devs[d])
+        later(src, z_send.at[step, d, i])
 
     def z_event(step, d, i):
         order = (PLUS, MINUS)[d]
@@ -205,28 +207,27 @@
         landed(tab_in.at[pl.ds(1, 7)], tab_sem.at[1])
         to_scalars(tab_in, 1, 7)
 
-    def pick(step, k):
-        source, xr, box = chunk(step, k), xs[step], outs[step]
-
-        def block(p, s):
-            number = tab_sm[k, 0, step * 256 + p * 64 + s * 32]
-            return source[jnp.maximum(number, 0)]
-
-        sems = (y_send.at[step, k], x_recv.at[step, k])
-        box[k, 2] = block(2, 0)
-        send(box.at[k, 2], relays[step].at[k, 0], sems[0], r_recv.at[step, k, 0], y_up)
-        box[k, 3] = block(2, 1)
-        send(box.at[k, 3], relays[step].at[k, 1], sems[0], r_recv.at[step, k, 1], y_down)
+    def block(step, k, p, s):
+        number = tab_sm[k, 0, step * 256 + p * 64 + s * 32]
+        return chunk(step, k)[jnp.maximum(number, 0)]
+
+    def pr(step, k):
+        for s, dev in enumerate((y_up, y_down)):
+            box = outs[step].at[k, 2 + s]
+            box[...] = block(step, k, 2, s)
+            send(box, relays[step].at[k, s], y_send.at[step, k], r_recv.at[step, k, s], dev)
+
+    def pp(step, k):
+        xr, box = xs[step], outs[step]
         for p, dev in ((1, y_up), (3, y_down)):
             first = 0 if p == 1 else 4
-            box[k, first] = block(p, 0)
-            box[k, first + 1] = block(p, 1)
-            send(
-                box.at[k, pl.ds(first, 2)], xr.at[pl.ds(k * 8 + p * 2, 2)], sems[0], sems[1], dev
-            )
-        later(box.at[k], sems[0])
-        xr[k * 8] = block(0, 0)
-        xr[k * 8 + 1] = block(0, 1)
+            for s in range(2):
+                box[k, first + s] = block(step, k, p, s)
+            there = xr.at[pl.ds(k * 8 + p * 2, 2)]
+            send(box.at[k, pl.ds(first, 2)], there, y_send.at[step, k], x_recv.at[step, k], dev)
+        later(box.at[k], y_send.at[step, k])
+        for s in range(2):
+            xr[k * 8 + s] = block(step, k, 0, s)
 
     def relay(step, k):
         for s, dev in enumerate((y_up, y_down)):
@@ -331,7 +332,7 @@
         out = sent_parts[step]
         for i in range(2):
             out[i * 8 : i * 8 + 8, :] = packed[i]
-        for j in range(1, NZ):
+        for j in (4, 3, 5, 2, 6, 1, 7):
             send(
                 out,
                 parts_in[step].at[j],
@@ -419,6 +420,8 @@
             sems = dp_send.at[4 + 4 * i + n], dp_recv.at[4 + 4 * i + n]
             send(phold.at[n, part, :], h1.at[i, n], sems[0], sems[1], dev)
             later(h1.at[i, n], sems[0])
+
+    def re(n):
         for at in (xp, xm, x):
             near = rows64(at)
             phold[n, near, :] = phold[n, near, :] + precv[n, near, :]
@@ -456,13 +459,18 @@
         norm = jnp.sqrt(square + 1e-06)
         for n in range(4):
             cur1[mine, n * 256 : (n + 1) * 256] = (v[n] / norm).astype(BF16)
-        pieces = ((0, dev_xp, 20), (32, dev_xm, 21), (32, dev_xp, 22), (0, dev_xm, 23))
-        for i, (shift, dev, sem) in enumerate(pieces):
-            part = cur1.at[cur_rows(core, x, 32, shift)]
+        own_rows(0)
+        to_core(cur1.at[mine], 24, 0)
+
+    def own_rows(second):
+        for i, (shift, dev) in enumerate(((0, dev_xp), (32, dev_xm))):
+            part = cur1.at[cur_rows(core, x, 32, 32 - shift if second else shift)]
+            sem = 20 + 2 * second + i
             send(part, part, dp_send.at[sem], dp_recv.at[sem], dev)
             later(part, dp_send.at[sem])
-            if i == 1:
-                to_core(cur1.at[mine], 24, 0)
+
+    def ub():
+        own_rows(1)
 
     def to_core(part, sem, group):
         send(part, part, dp_send.at[sem], dp_recv.at[26 + group], dev_core)
@@ -567,7 +575,10 @@
     parts = dict(
         zs=z_start,
         ze=z_event,
-        pick=pick,
+        pr=pr,
+        pp=pp,
+        re=re,
+        ub=ub,
         relay=relay,
         score=score,
         share=share,
@@ -593,13 +604,15 @@
         fin=fin,
     )
     for name, *numbers in SCHEDULE:
-        parts[name](*numbers)
-        if (name, *numbers) == ("zs", 0, 0):
+        if (name, *numbers) == ("pr", 0, 0):
             tables()
             for load in loads:
                 load.wait()
+        parts[name](*numbers)
         if (name, *numbers) == ("relay", 0, 0):
             tables_in()
+        if (name, *numbers) in (("share", 1), ("whole", 1)):
+            drain()
 
 
 def on_device(points, candidates, centroids):
@@ -663,7 +676,7 @@
             sem((2,)),
         ],
         compiler_params=pltpu.CompilerParams(
-            collective_id=0, has_side_effects=True, vmem_limit_bytes=56 * 1024 * 1024
+            collective_id=0, has_side_effects=True, vmem_limit_bytes=54250 * 1024
         ),
     )(points.reshape(steps, NB, PB, D), jnp.transpose(candidates, (0, 2, 1)), centroids)
     return sums, counts.reshape(CBS)

time: 141 us -> 139 us (0.986)
  Pallas kernels: 138 us -> 136 us
    pallas_call x1, Pallas kernels: 138 us -> 136 us  [on_device(): pl.pallas_call(kernel, out_shape=(jax.ShapeDtypeStruct((CBS, D // (NX * N...]
where the time goes in v5:
time: 139 us; the launch traced here: 138 us
  Pallas kernels  136 us (98%)
  local copies, waits for them, and re-layouts  1.96 us (1%)
    pallas_call x1, Pallas kernels, on_device(): pl.pallas_call(kernel, out_shape=(jax.ShapeDtypeStruct((CBS, D // (NX * N...  136 us

profile of v5, /device:TPU:2, one launch (start us, length us, event | category | flops | bytes accessed | tf_op | source)
XLA Modules:
  0.0 138.2 jit_solution(9923026288853794814)
XLA Ops:
  0.6 0.0 copy-start
  0.6 0.7 copy-done
  1.3 135.6 %shard_map.50 = (f32[512,128]{1,0:T(8,128)S(1)}, f32[4,128]{1,0:T(4,128)S(1)}) custom-call(bf16[2,8,32,1024]{3,2,1,0:T(8,128)(2,1)} %bitcast.5, s32[2,4,8]{2,1,0:T(4,128)S(1)} %bitcast.3, bf16[512,1024]{1,0:T(8,128)(2,1)} %cent_hbm.1), custom_call_target="tpu_custom_call" | custom-call | tf_op jit(solution)/shard_map/pallas_call | solution.py:622
  136.9 0.7 copy.7
  137.6 0.6 copy.8
Async XLA Ops:
  0.6 0.7 copy-start

commit v6 on v5

--- a/solution.py
+++ b/solution.py
@@ -158,8 +158,7 @@
         k, h = (PLUS, MINUS)[d][i]
         src = half(pts_hbm.at[step], h)
         dst = half(chunk(step, k), h)
-        send(src, dst, z_send.at[step, d, i], z_recv.at[step, d, i], z_devs[d])
-        later(src, z_send.at[step, d, i])
+        send(src, dst, z_send.at[step], z_recv.at[step, d, i], z_devs[d])
 
     def z_event(step, d, i):
         order = (PLUS, MINUS)[d]
@@ -168,8 +167,7 @@
         landed(here, z_recv.at[step, d, i])
         if i < 5:
             dst = half(chunk(step, order[i + 2][0]), h)
-            send(here, dst, z_send.at[step, d, i + 2], z_recv.at[step, d, i + 2], z_devs[d])
-            later(here, z_send.at[step, d, i + 2])
+            send(here, dst, z_send.at[step], z_recv.at[step, d, i + 2], z_devs[d])
 
     def tables():
         row = lax.broadcasted_iota(jnp.int32, (8, 128), 0)
@@ -215,7 +213,7 @@
         for s, dev in enumerate((y_up, y_down)):
             box = outs[step].at[k, 2 + s]
             box[...] = block(step, k, 2, s)
-            send(box, relays[step].at[k, s], y_send.at[step, k], r_recv.at[step, k, s], dev)
+            send(box, relays[step].at[k, s], y_send.at[step], r_recv.at[step, k], dev)
 
     def pp(step, k):
         xr, box = xs[step], outs[step]
@@ -224,23 +222,20 @@
             for s in range(2):
                 box[k, first + s] = block(step, k, p, s)
             there = xr.at[pl.ds(k * 8 + p * 2, 2)]
-            send(box.at[k, pl.ds(first, 2)], there, y_send.at[step, k], x_recv.at[step, k], dev)
-        later(box.at[k], y_send.at[step, k])
+            send(box.at[k, pl.ds(first, 2)], there, y_send.at[step], x_recv.at[step, k], dev)
         for s in range(2):
             xr[k * 8 + s] = block(step, k, 0, s)
 
     def relay(step, k):
+        landed(relays[step].at[k], r_recv.at[step, k])
         for s, dev in enumerate((y_up, y_down)):
-            here = relays[step].at[k, s]
-            landed(here, r_recv.at[step, k, s])
-            send(
-                here,
-                xs[step].at[k * 8 + 4 + s],
-                r_send.at[step, k],
-                x_recv.at[step, k],
-                dev,
-            )
-        later(relays[step].at[k], r_send.at[step, k])
+            here, there = relays[step].at[k, s], xs[step].at[k * 8 + 4 + s]
+            send(here, there, r_send.at[step], x_recv.at[step, k], dev)
+
+    def points_sent(step):
+        landed(xs[step].at[pl.ds(0, 56)], z_send.at[step])
+        landed(outs[step], y_send.at[step])
+        landed(relays[step], r_send.at[step])
 
     def arrived(step, k):
         landed(xs[step].at[pl.ds(k * 8 + 2, 6)], x_recv.at[step, k])
@@ -405,8 +400,7 @@
 
     def rf(n):
         psend[n] = half_sums(1 - core, n)
-        send(psend.at[n], precv.at[n], dp_send.at[n], dp_recv.at[n], dev_core)
-        later(psend.at[n], dp_send.at[n])
+        send(psend.at[n], precv.at[n], dp_send.at[0], dp_recv.at[n], dev_core)
 
     def ro(n):
         phold[n] = half_sums(core, n)
@@ -417,9 +411,7 @@
         phold[n, far, :] = phold[n, far, :] + precv[n, far, :]
         sides = ((rows64(xo, 32), dev_xp), (rows64(xo, 32, 32), dev_xm))
         for i, (part, dev) in enumerate(sides):
-            sems = dp_send.at[4 + 4 * i + n], dp_recv.at[4 + 4 * i + n]
-            send(phold.at[n, part, :], h1.at[i, n], sems[0], sems[1], dev)
-            later(h1.at[i, n], sems[0])
+            send(phold.at[n, part, :], h1.at[i, n], dp_send.at[1], dp_recv.at[4 + n], dev)
 
     def re(n):
         for at in (xp, xm, x):
@@ -429,25 +421,21 @@
             second_hop(n, i, at, shift, dev)
 
     def second_hop(n, i, at, shift, dev):
-        sems = dp_send.at[12 + 4 * i + n], dp_recv.at[12 + 4 * i + n]
         src = phold.at[n, rows64(at, 32, shift), :]
-        send(src, h2.at[i, n, pl.ds(shift, 32)], sems[0], sems[1], dev)
+        send(src, h2.at[i, n, pl.ds(shift, 32)], dp_send.at[2], dp_recv.at[8], dev)
 
     def rh(n):
+        landed(h2.at[0, n], dp_recv.at[4 + n])
         for i, (at, shift, dev) in enumerate(((xp, 0, dev_xp), (xm, 32, dev_xm))):
-            landed(h1.at[i, n], dp_recv.at[4 + 4 * i + n])
             part = rows64(at, 32, shift)
             phold[n, part, :] = phold[n, part, :] + h1[i, n]
             second_hop(n, i, at, shift, dev)
-            later(h2.at[i, n], dp_send.at[12 + 4 * i + n])
 
     def cur_rows(which_core, at, count=64, shift=0):
         return pl.ds(pl.multiple_of(which_core * 256 + at * 64 + shift, 32), count)
 
     def update():
-        for n in range(4):
-            landed(h2.at[0, n], dp_recv.at[12 + n])
-            landed(h2.at[1, n], dp_recv.at[16 + n])
+        landed(h2, dp_recv.at[8])
         own = rows64(x)
         mine = cur_rows(core, x)
         v = [
@@ -460,44 +448,40 @@
         for n in range(4):
             cur1[mine, n * 256 : (n + 1) * 256] = (v[n] / norm).astype(BF16)
         own_rows(0)
-        to_core(cur1.at[mine], 24, 0)
+        to_core(cur1.at[mine], 0)
 
     def own_rows(second):
         for i, (shift, dev) in enumerate(((0, dev_xp), (32, dev_xm))):
             part = cur1.at[cur_rows(core, x, 32, 32 - shift if second else shift)]
-            sem = 20 + 2 * second + i
-            send(part, part, dp_send.at[sem], dp_recv.at[sem], dev)
-            later(part, dp_send.at[sem])
+            send(part, part, dp_send.at[3], dp_recv.at[9 + 2 * second + i], dev)
 
     def ub():
         own_rows(1)
 
-    def to_core(part, sem, group):
-        send(part, part, dp_send.at[sem], dp_recv.at[26 + group], dev_core)
-        later(part, dp_send.at[sem])
+    def to_core(part, group):
+        send(part, part, dp_send.at[3], dp_recv.at[15 + group], dev_core)
 
     def gather1():
         for i, (at, shift, dev) in enumerate(((xm, 0, dev_xp), (xp, 32, dev_xm))):
             part = cur1.at[cur_rows(core, at, 32, shift)]
-            landed(part, dp_recv.at[20 + i])
-            send(part, part, dp_send.at[25 + i], dp_recv.at[24 + i], dev)
-            later(part, dp_send.at[25 + i])
-            to_core(part, 27 + i, 1)
+            landed(part, dp_recv.at[9 + i])
+            send(part, part, dp_send.at[3], dp_recv.at[13 + i], dev)
+            to_core(part, 1)
 
     def gather1b():
         for i, (at, shift) in enumerate(((xm, 32), (xp, 0))):
             part = cur1.at[cur_rows(core, at, 32, shift)]
-            landed(part, dp_recv.at[22 + i])
-            to_core(part, 29 + i, 1)
+            landed(part, dp_recv.at[11 + i])
+            to_core(part, 1)
 
     def gather2():
         for i, shift in enumerate((0, 32)):
             part = cur1.at[cur_rows(core, xo, 32, shift)]
-            landed(part, dp_recv.at[24 + i])
-            to_core(part, 31 + i, 2)
+            landed(part, dp_recv.at[13 + i])
+            to_core(part, 2)
 
     def gw(group):
-        landed(cur1.at[pl.ds(0, (64, 128, 64)[group])], dp_recv.at[26 + group])
+        landed(cur1.at[pl.ds(0, (64, 128, 64)[group])], dp_recv.at[15 + group])
 
     def ls(j):
         lanes = pl.ds(pl.multiple_of((xo, xp, xm, x)[j] * 256, 256), 256)
@@ -518,12 +502,11 @@
         g[0] = both(0).astype(BF16)
         for i, dev in enumerate((dev_xp, dev_xm)):
             rows = pl.ds(256 * i, 256)
-            send(g.at[0, rows], q.at[i], fin_send.at[2 + i], fin_recv.at[5 + i], dev)
-            later(q.at[i], fin_send.at[2 + i])
+            send(g.at[0, rows], q.at[i], fin_send.at[2], fin_recv.at[5 + i], dev)
 
     def last_hop(i, rows):
         dev = (dev_xp, dev_xm)[i]
-        send(g.at[1 + i, rows], u.at[i, rows], fin_send.at[4 + i], fin_recv.at[7 + i], dev)
+        send(g.at[1 + i, rows], u.at[i, rows], fin_send.at[3], fin_recv.at[7 + i], dev)
 
     def lv():
         for i in range(2):
@@ -539,7 +522,6 @@
             rows = pl.ds(256 * i, 256)
             g[1 + i, rows] = (fb[1 + i, core, rows, :] + q[i].astype(F32)).astype(BF16)
             last_hop(i, rows)
-            later(u.at[i], fin_send.at[4 + i])
 
     def cnt():
         ones = jnp.ones((8, 64 * PB), BF16)
@@ -566,10 +548,12 @@
         for j in range(4):
             out_counts[j : j + 1, :] = count[:, j * 128 : (j + 1) * 128]
         drain()
+        landed(q, fin_send.at[2])
 
     def fin():
         landed(u.at[0], fin_recv.at[7])
         landed(u.at[1], fin_recv.at[8])
+        landed(u, fin_send.at[3])
         out_sums[...] = fb[3, core] + (u[0].astype(F32) + u[1].astype(F32))
 
     parts = dict(
@@ -611,8 +595,13 @@
         parts[name](*numbers)
         if (name, *numbers) == ("relay", 0, 0):
             tables_in()
-        if (name, *numbers) in (("share", 1), ("whole", 1)):
-            drain()
+        if (name, *numbers) == ("partial", 1):
+            points_sent(0)
+            points_sent(1)
+            landed(psend, dp_send.at[0])
+            landed(h1, dp_send.at[1])
+            landed(h2, dp_send.at[2])
+            landed(cur1.at[pl.ds(0, 448)], dp_send.at[3])
 
 
 def on_device(points, candidates, centroids):
@@ -661,17 +650,17 @@
             pltpu.VMEM((2, 256, 128), BF16),
             pltpu.VMEM((2, CBS, 128), BF16),
             pltpu.VMEM((NX * NC, 1, CBS), F32),
+            sem((steps,)),
             sem((steps, 2, 7)),
-            sem((steps, 2, 7)),
+            sem((steps,)),
             sem((steps, NZ)),
             sem((steps, NZ)),
-            sem((steps, NZ, 2)),
-            sem((steps, NZ)),
+            sem((steps,)),
             sem((steps, 6)),
             sem((3,)),
-            sem((33,)),
-            sem((29,)),
-            sem((6,)),
+            sem((4,)),
+            sem((18,)),
+            sem((4,)),
             sem((9,)),
             sem((2,)),
         ],

time: 139 us -> 138 us (level)
  no operation moved by 1% of the time
where the time goes in v6:
time: 138 us; the launch traced here: 137 us
  Pallas kernels  135 us (98%)
  local copies, waits for them, and re-layouts  1.96 us (1%)
    pallas_call x1, Pallas kernels, on_device(): pl.pallas_call(kernel, out_shape=(jax.ShapeDtypeStruct((CBS, D // (NX * N...  135 us

profile of v6, /device:TPU:2, one launch (start us, length us, event | category | flops | bytes accessed | tf_op | source)
XLA Modules:
  0.0 137.4 jit_solution(4985855532917733387)
XLA Ops:
  0.6 0.0 copy-start
  0.6 0.7 copy-done
  1.3 134.8 %shard_map.50 = (f32[512,128]{1,0:T(8,128)S(1)}, f32[4,128]{1,0:T(4,128)S(1)}) custom-call(bf16[2,8,32,1024]{3,2,1,0:T(8,128)(2,1)} %bitcast.5, s32[2,4,8]{2,1,0:T(4,128)S(1)} %bitcast.3, bf16[512,1024]{1,0:T(8,128)(2,1)} %cent_hbm.1), custom_call_target="tpu_custom_call" | custom-call | tf_op jit(solution)/shard_map/pallas_call | solution.py:611
  136.1 0.7 copy.7
  136.9 0.6 copy.8
Async XLA Ops:
  0.6 0.7 copy-start

commit v7 on v6

--- a/solution.py
+++ b/solution.py
@@ -14,26 +14,26 @@
 PLUS = ((1, 0), (1, 1), (2, 0), (2, 1), (3, 0), (3, 1), (4, 0))
 MINUS = ((7, 1), (7, 0), (6, 1), (6, 0), (5, 1), (5, 0), (4, 1))
 SCHEDULE = (
-    ("zs", 0, 0, 0), ("pr", 0, 0), ("zs", 0, 0, 1), ("pp", 0, 0), ("pr", 1, 0), ("pp", 1, 0), ("zs", 0, 1, 0),
-    ("relay", 0, 0), ("zs", 0, 1, 1), ("relay", 1, 0), ("ze", 0, 0, 0), ("ze", 0, 1, 0), ("ze", 0, 0, 1), ("pr", 0, 1),
-    ("pp", 0, 1), ("ze", 0, 1, 1), ("pr", 0, 7), ("pp", 0, 7), ("ze", 0, 0, 2), ("relay", 0, 1), ("relay", 0, 7),
-    ("ze", 0, 1, 2), ("ze", 0, 0, 3), ("pr", 0, 2), ("pp", 0, 2), ("score", 1), ("score", 0), ("ze", 0, 1, 3),
-    ("pr", 0, 6), ("relay", 0, 2), ("pp", 0, 6), ("ze", 0, 0, 4), ("relay", 0, 6), ("score", 7), ("ze", 0, 1, 4),
-    ("ze", 0, 0, 5), ("pr", 0, 3), ("pp", 0, 3), ("ze", 0, 1, 5), ("score", 2), ("zs", 1, 0, 0), ("pr", 0, 5),
-    ("zs", 1, 1, 0), ("relay", 0, 3), ("pp", 0, 5), ("score", 6), ("zs", 1, 1, 1), ("ze", 0, 1, 6), ("ze", 0, 0, 6),
-    ("pr", 0, 4), ("zs", 1, 0, 1), ("relay", 0, 5), ("pp", 0, 4), ("score", 3), ("relay", 0, 4), ("ze", 1, 0, 0),
+    ("zs", 0, 0, 0), ("zs", 0, 1, 0), ("pr", 0, 0), ("pp", 0, 0), ("pr", 1, 0), ("pp", 1, 0), ("zs", 0, 0, 1),
+    ("zs", 0, 1, 1), ("ze", 0, 0, 0), ("relay", 0, 0), ("relay", 1, 0), ("ze", 0, 1, 0), ("ze", 0, 0, 1), ("pr", 0, 1),
+    ("ze", 0, 1, 1), ("pr", 0, 7), ("pp", 0, 7), ("relay", 0, 1), ("pp", 0, 1), ("relay", 0, 7), ("ze", 0, 0, 2),
+    ("ze", 0, 1, 2), ("ze", 0, 0, 3), ("pr", 0, 2), ("pp", 0, 2), ("score", 7), ("score", 1), ("ze", 0, 1, 3),
+    ("pr", 0, 6), ("pp", 0, 6), ("score", 0), ("ze", 0, 1, 4), ("relay", 0, 2), ("relay", 0, 6), ("ze", 0, 0, 4),
+    ("ze", 0, 0, 5), ("pr", 0, 3), ("pp", 0, 3), ("ze", 0, 1, 5), ("pr", 0, 5), ("zs", 1, 0, 0), ("pp", 0, 5),
+    ("zs", 1, 1, 0), ("ze", 0, 1, 6), ("ze", 0, 0, 6), ("pr", 0, 4), ("relay", 0, 3), ("score", 2), ("pp", 0, 4),
+    ("zs", 1, 1, 1), ("zs", 1, 0, 1), ("score", 6), ("relay", 0, 5), ("ze", 1, 0, 0), ("relay", 0, 4), ("score", 3),
     ("ze", 1, 1, 0), ("score", 5), ("ze", 1, 1, 1), ("pr", 1, 7), ("pp", 1, 7), ("score", 4), ("share", 0),
-    ("ze", 1, 0, 1), ("pr", 1, 1), ("pp", 1, 1), ("partial", 0), ("relay", 1, 7), ("ze", 1, 1, 2), ("ze", 1, 0, 2),
-    ("relay", 1, 1), ("whole", 0), ("ze", 1, 1, 3), ("pr", 1, 6), ("pp", 1, 6), ("ze", 1, 0, 3), ("pr", 1, 2),
-    ("pp", 1, 2), ("weigh", 0), ("rf", 0), ("ro", 0), ("rf", 1), ("ro", 1), ("rf", 2), ("ro", 2), ("rc", 0), ("re", 0),
-    ("rf", 3), ("rc", 1), ("re", 1), ("relay", 1, 6), ("rc", 2), ("relay", 1, 2), ("re", 2), ("ro", 3), ("rc", 3),
-    ("re", 3), ("ze", 1, 1, 4), ("ze", 1, 0, 4), ("ze", 1, 1, 5), ("pr", 1, 5), ("rh", 1), ("pp", 1, 5), ("rh", 0),
-    ("rh", 2), ("ze", 1, 0, 5), ("rh", 3), ("pr", 1, 3), ("pp", 1, 3), ("update",), ("ze", 1, 0, 6), ("ze", 1, 1, 6),
-    ("ub",), ("gw", 0), ("sc", 0, 6), ("relay", 1, 3), ("sc", 0, 7), ("sc", 0, 2), ("sc", 0, 0), ("gather1",),
-    ("gather1b",), ("pr", 1, 4), ("sc", 0, 1), ("relay", 1, 5), ("pp", 1, 4), ("sc", 0, 3), ("gw", 1), ("sc", 1, 6),
-    ("sc", 1, 0), ("gather2",), ("sc", 1, 2), ("sc", 1, 1), ("sc", 1, 3), ("relay", 1, 4), ("sc", 1, 7), ("gw", 2),
-    ("sc", 2, 2), ("sc", 2, 1), ("sc", 0, 5), ("sc", 1, 5), ("sc", 2, 3), ("sc", 2, 0), ("sc", 2, 7), ("sc", 2, 5),
-    ("sc", 0, 4), ("sc", 2, 4), ("sc", 1, 4), ("sc", 2, 6), ("share", 1), ("partial", 1), ("whole", 1), ("weigh", 1),
+    ("ze", 1, 0, 1), ("pr", 1, 1), ("pp", 1, 1), ("relay", 1, 7), ("partial", 0), ("relay", 1, 1), ("ze", 1, 0, 2),
+    ("ze", 1, 1, 2), ("whole", 0), ("ze", 1, 0, 3), ("ze", 1, 1, 3), ("pr", 1, 2), ("pp", 1, 2), ("pr", 1, 6),
+    ("pp", 1, 6), ("weigh", 0), ("rf", 0), ("ro", 0), ("rf", 1), ("ro", 1), ("rf", 2), ("ro", 2), ("rc", 0), ("re", 0),
+    ("rf", 3), ("rc", 1), ("rc", 2), ("re", 1), ("ze", 1, 0, 4), ("relay", 1, 6), ("re", 2), ("ro", 3), ("rc", 3),
+    ("relay", 1, 2), ("rh", 1), ("ze", 1, 1, 4), ("ze", 1, 0, 5), ("pr", 1, 3), ("re", 3), ("rh", 0), ("pp", 1, 3),
+    ("ze", 1, 1, 5), ("pr", 1, 5), ("rh", 2), ("rh", 3), ("update",), ("pp", 1, 5), ("ze", 1, 1, 6), ("ub",),
+    ("gw", 0), ("sc", 0, 7), ("sc", 0, 2), ("sc", 0, 0), ("ze", 1, 0, 6), ("relay", 1, 3), ("pr", 1, 4), ("gather1",),
+    ("gather1b",), ("sc", 0, 1), ("pp", 1, 4), ("sc", 0, 6), ("relay", 1, 5), ("gw", 1), ("sc", 1, 6), ("sc", 1, 1),
+    ("gather2",), ("sc", 1, 7), ("sc", 1, 0), ("sc", 1, 2), ("sc", 0, 3), ("relay", 1, 4), ("gw", 2), ("sc", 2, 3),
+    ("sc", 2, 1), ("sc", 1, 3), ("sc", 2, 7), ("sc", 0, 5), ("sc", 1, 5), ("sc", 2, 6), ("sc", 2, 5), ("sc", 2, 2),
+    ("sc", 2, 0), ("sc", 0, 4), ("sc", 1, 4), ("sc", 2, 4), ("share", 1), ("partial", 1), ("whole", 1), ("weigh", 1),
     ("ls", 0), ("ls", 1), ("ls", 2), ("lq",), ("ls", 3), ("lv",), ("cnt",), ("lu",), ("own",), ("fin",),
 )
 

time: 138 us -> 137 us (level)
  no operation moved by 1% of the time
where the time goes in v7:
time: 137 us
  Pallas kernels  134 us (98%)
  local copies, waits for them, and re-layouts  1.96 us (1%)
    pallas_call x1, Pallas kernels, on_device(): pl.pallas_call(kernel, out_shape=(jax.ShapeDtypeStruct((CBS, D // (NX * N...  134 us

profile of v7, /device:TPU:2, one launch (start us, length us, event | category | flops | bytes accessed | tf_op | source)
XLA Modules:
  0.0 136.8 jit_solution(14846373801455331956)
XLA Ops:
  0.6 0.0 copy-start
  0.6 0.7 copy-done
  1.3 134.2 %shard_map.50 = (f32[512,128]{1,0:T(8,128)S(1)}, f32[4,128]{1,0:T(4,128)S(1)}) custom-call(bf16[2,8,32,1024]{3,2,1,0:T(8,128)(2,1)} %bitcast.5, s32[2,4,8]{2,1,0:T(4,128)S(1)} %bitcast.3, bf16[512,1024]{1,0:T(8,128)(2,1)} %cent_hbm.1), custom_call_target="tpu_custom_call" | custom-call | tf_op jit(solution)/shard_map/pallas_call | solution.py:611
  135.5 0.7 copy.7
  136.2 0.6 copy.8
Async XLA Ops:
  0.6 0.7 copy-start

commit v8 on v7

--- a/solution.py
+++ b/solution.py
@@ -14,27 +14,27 @@
 PLUS = ((1, 0), (1, 1), (2, 0), (2, 1), (3, 0), (3, 1), (4, 0))
 MINUS = ((7, 1), (7, 0), (6, 1), (6, 0), (5, 1), (5, 0), (4, 1))
 SCHEDULE = (
-    ("zs", 0, 0, 0), ("zs", 0, 1, 0), ("pr", 0, 0), ("pp", 0, 0), ("pr", 1, 0), ("pp", 1, 0), ("zs", 0, 0, 1),
-    ("zs", 0, 1, 1), ("ze", 0, 0, 0), ("relay", 0, 0), ("relay", 1, 0), ("ze", 0, 1, 0), ("ze", 0, 0, 1), ("pr", 0, 1),
+    ("zs", 0, 0, 0), ("zs", 0, 1, 0), ("pr", 0, 0), ("pp", 0, 0), ("zs", 0, 0, 1), ("pr", 1, 0), ("pp", 1, 0),
+    ("zs", 0, 1, 1), ("relay", 1, 0), ("relay", 0, 0), ("ze", 0, 0, 0), ("ze", 0, 1, 0), ("ze", 0, 0, 1), ("pr", 0, 1),
     ("ze", 0, 1, 1), ("pr", 0, 7), ("pp", 0, 7), ("relay", 0, 1), ("pp", 0, 1), ("relay", 0, 7), ("ze", 0, 0, 2),
-    ("ze", 0, 1, 2), ("ze", 0, 0, 3), ("pr", 0, 2), ("pp", 0, 2), ("score", 7), ("score", 1), ("ze", 0, 1, 3),
-    ("pr", 0, 6), ("pp", 0, 6), ("score", 0), ("ze", 0, 1, 4), ("relay", 0, 2), ("relay", 0, 6), ("ze", 0, 0, 4),
-    ("ze", 0, 0, 5), ("pr", 0, 3), ("pp", 0, 3), ("ze", 0, 1, 5), ("pr", 0, 5), ("zs", 1, 0, 0), ("pp", 0, 5),
-    ("zs", 1, 1, 0), ("ze", 0, 1, 6), ("ze", 0, 0, 6), ("pr", 0, 4), ("relay", 0, 3), ("score", 2), ("pp", 0, 4),
-    ("zs", 1, 1, 1), ("zs", 1, 0, 1), ("score", 6), ("relay", 0, 5), ("ze", 1, 0, 0), ("relay", 0, 4), ("score", 3),
+    ("ze", 0, 1, 2), ("ze", 0, 0, 3), ("pr", 0, 2), ("pp", 0, 2), ("score", 1), ("ze", 0, 1, 3), ("pr", 0, 6),
+    ("pp", 0, 6), ("score", 0), ("relay", 0, 2), ("ze", 0, 1, 4), ("relay", 0, 6), ("ze", 0, 0, 4), ("ze", 0, 0, 5),
+    ("pr", 0, 3), ("pp", 0, 3), ("ze", 0, 1, 5), ("pr", 0, 5), ("zs", 1, 0, 0), ("pp", 0, 5), ("zs", 1, 1, 0),
+    ("score", 7), ("ze", 0, 0, 6), ("ze", 0, 1, 6), ("zs", 1, 0, 1), ("pr", 0, 4), ("relay", 0, 3), ("relay", 0, 5),
+    ("score", 2), ("pp", 0, 4), ("zs", 1, 1, 1), ("score", 6), ("relay", 0, 4), ("ze", 1, 0, 0), ("score", 3),
     ("ze", 1, 1, 0), ("score", 5), ("ze", 1, 1, 1), ("pr", 1, 7), ("pp", 1, 7), ("score", 4), ("share", 0),
-    ("ze", 1, 0, 1), ("pr", 1, 1), ("pp", 1, 1), ("relay", 1, 7), ("partial", 0), ("relay", 1, 1), ("ze", 1, 0, 2),
-    ("ze", 1, 1, 2), ("whole", 0), ("ze", 1, 0, 3), ("ze", 1, 1, 3), ("pr", 1, 2), ("pp", 1, 2), ("pr", 1, 6),
-    ("pp", 1, 6), ("weigh", 0), ("rf", 0), ("ro", 0), ("rf", 1), ("ro", 1), ("rf", 2), ("ro", 2), ("rc", 0), ("re", 0),
-    ("rf", 3), ("rc", 1), ("rc", 2), ("re", 1), ("ze", 1, 0, 4), ("relay", 1, 6), ("re", 2), ("ro", 3), ("rc", 3),
-    ("relay", 1, 2), ("rh", 1), ("ze", 1, 1, 4), ("ze", 1, 0, 5), ("pr", 1, 3), ("re", 3), ("rh", 0), ("pp", 1, 3),
-    ("ze", 1, 1, 5), ("pr", 1, 5), ("rh", 2), ("rh", 3), ("update",), ("pp", 1, 5), ("ze", 1, 1, 6), ("ub",),
-    ("gw", 0), ("sc", 0, 7), ("sc", 0, 2), ("sc", 0, 0), ("ze", 1, 0, 6), ("relay", 1, 3), ("pr", 1, 4), ("gather1",),
-    ("gather1b",), ("sc", 0, 1), ("pp", 1, 4), ("sc", 0, 6), ("relay", 1, 5), ("gw", 1), ("sc", 1, 6), ("sc", 1, 1),
-    ("gather2",), ("sc", 1, 7), ("sc", 1, 0), ("sc", 1, 2), ("sc", 0, 3), ("relay", 1, 4), ("gw", 2), ("sc", 2, 3),
-    ("sc", 2, 1), ("sc", 1, 3), ("sc", 2, 7), ("sc", 0, 5), ("sc", 1, 5), ("sc", 2, 6), ("sc", 2, 5), ("sc", 2, 2),
-    ("sc", 2, 0), ("sc", 0, 4), ("sc", 1, 4), ("sc", 2, 4), ("share", 1), ("partial", 1), ("whole", 1), ("weigh", 1),
-    ("ls", 0), ("ls", 1), ("ls", 2), ("lq",), ("ls", 3), ("lv",), ("cnt",), ("lu",), ("own",), ("fin",),
+    ("ze", 1, 0, 1), ("pr", 1, 1), ("pp", 1, 1), ("partial", 0), ("relay", 1, 7), ("relay", 1, 1), ("ze", 1, 0, 2),
+    ("ze", 1, 1, 2), ("whole", 0), ("ze", 1, 0, 3), ("pr", 1, 2), ("pp", 1, 2), ("ze", 1, 1, 3), ("pr", 1, 6),
+    ("pp", 1, 6), ("wa",), ("rf", 0), ("wb",), ("ro", 0), ("rf", 1), ("ro", 1), ("rf", 2), ("ro", 2), ("rc", 0),
+    ("re", 0), ("rf", 3), ("rc", 1), ("re", 1), ("relay", 1, 2), ("rc", 2), ("re", 2), ("ro", 3), ("rc", 3),
+    ("ze", 1, 0, 4), ("ze", 1, 0, 5), ("pr", 1, 3), ("ze", 1, 1, 4), ("rh", 0), ("re", 3), ("rh", 1), ("relay", 1, 6),
+    ("rh", 2), ("pp", 1, 3), ("rh", 3), ("relay", 1, 3), ("update",), ("ze", 1, 1, 5), ("pr", 1, 5), ("ze", 1, 1, 6),
+    ("ub",), ("pp", 1, 5), ("gw", 0), ("sc", 0, 0), ("sc", 0, 7), ("sc", 0, 6), ("ze", 1, 0, 6), ("pr", 1, 4),
+    ("gather1",), ("gather1b",), ("sc", 0, 3), ("relay", 1, 5), ("sc", 0, 1), ("pp", 1, 4), ("sc", 0, 2), ("gw", 1),
+    ("sc", 1, 0), ("sc", 1, 2), ("gather2",), ("sc", 1, 3), ("sc", 1, 6), ("relay", 1, 4), ("sc", 1, 7), ("sc", 1, 1),
+    ("gw", 2), ("sc", 2, 2), ("sc", 2, 3), ("sc", 2, 1), ("sc", 2, 0), ("sc", 2, 7), ("sc", 0, 5), ("sc", 2, 6),
+    ("sc", 2, 5), ("sc", 1, 5), ("sc", 0, 4), ("sc", 2, 4), ("sc", 1, 4), ("share", 1), ("partial", 1), ("whole", 1),
+    ("weigh",), ("ls", 0), ("ls", 1), ("ls", 2), ("lq",), ("ls", 3), ("lv",), ("cnt",), ("lu",), ("own",), ("fin",),
 )
 
 
@@ -372,18 +372,32 @@
             )
         later(back.at[pl.ds(1, 3)], st_sem.at[step, 4])
 
-    def weigh(step):
-        back = shifts[step]
-        landed(back.at[pl.ds(1, 3)], st_sem.at[step, 5])
+    def wa():
+        landed(shifts[0].at[pl.ds(1, 3)], st_sem.at[0, 5])
+        weigh_half(1 - core)
+
+    def wb():
+        weigh_half(core)
+
+    def weigh_half(which):
+        back = shifts[0]
+        rows = pl.ds(pl.multiple_of(which * 256, 256), 256)
+        for k in range(NZ):
+            for t in range(2):
+                shift = jnp.where(low, back[2 * t, k : k + 1, :], back[2 * t + 1, k : k + 1, :])
+                half_lanes = slice(t * 128, (t + 1) * 128)
+                scale = jnp.exp(tops[k, :, half_lanes] - shift)
+                lanes = pl.ds(k * 256 + t * 128, 128)
+                w[rows, lanes] = (scores[k, rows, half_lanes] * scale).astype(BF16)
+
+    def weigh():
+        back = shifts[1]
+        landed(back.at[pl.ds(1, 3)], st_sem.at[1, 5])
         for k in range(NZ):
             for t in range(2):
                 shift = jnp.where(low, back[2 * t, k : k + 1, :], back[2 * t + 1, k : k + 1, :])
                 lanes = pl.ds(k * 256 + t * 128, 128)
                 half_lanes = slice(t * 128, (t + 1) * 128)
-                if step == 0:
-                    scale = jnp.exp(tops[k, :, half_lanes] - shift)
-                    w[:, lanes] = (scores[k, :, half_lanes] * scale).astype(BF16)
-                    continue
                 for at in range(NX):
                     scale = jnp.exp(tops4[at, k, :, half_lanes] - shift)
                     for first in (at * 64, 256 + at * 64):
@@ -569,6 +583,8 @@
         partial=partial,
         whole=whole,
         weigh=weigh,
+        wa=wa,
+        wb=wb,
         rf=rf,
         ro=ro,
         rc=rc,

time: 137 us -> 137 us (level)
  no operation moved by 1% of the time
where the time goes in v8:
time: 137 us; the launch traced here: 136 us
  Pallas kernels  133 us (97%)
  local copies, waits for them, and re-layouts  1.96 us (1%)
    pallas_call x1, Pallas kernels, on_device(): pl.pallas_call(kernel, out_shape=(jax.ShapeDtypeStruct((CBS, D // (NX * N...  133 us

profile of v8, /device:TPU:2, one launch (start us, length us, event | category | flops | bytes accessed | tf_op | source)
XLA Modules:
  0.0 136.1 jit_solution(4436615574634130585)
XLA Ops:
  0.6 0.0 copy-start
  0.6 0.7 copy-done
  1.3 133.4 %shard_map.50 = (f32[512,128]{1,0:T(8,128)S(1)}, f32[4,128]{1,0:T(4,128)S(1)}) custom-call(bf16[2,8,32,1024]{3,2,1,0:T(8,128)(2,1)} %bitcast.5, s32[2,4,8]{2,1,0:T(4,128)S(1)} %bitcast.3, bf16[512,1024]{1,0:T(8,128)(2,1)} %cent_hbm.1), custom_call_target="tpu_custom_call" | custom-call | tf_op jit(solution)/shard_map/pallas_call | solution.py:627
  134.8 0.7 copy.7
  135.5 0.6 copy.8
Async XLA Ops:
  0.6 0.7 copy-start
